TPU v7x, 32 devices: a whole 2x2x4 slice. The times are simulated.
32 devices in a mesh: dp: 4 (over z), fsdp: 8 (over y, x, core).
Axes of the slice: x: 2, y: 2, z: 4, core: 2. Of those that a mesh axis runs over, the one named last changes fastest.
Arguments:
- tokens: bfloat16 [65536, 1280], P(('dp', 'fsdp')), may hold values from -6 to 6
- cotangent: bfloat16 [65536, 1280], P(('dp', 'fsdp')), may hold values from -6 to 6
- lengths: int32 [64], P(('dp', 'fsdp')), may hold values from 256 to 1024, as said below
- labels: int32 [65536], P(('dp', 'fsdp')), may hold values from 0 to 24
- w_in: float32 [1280, 640], P('dp', 'fsdp'), may hold values from -0.15625 to 0.15625
- w_conv: float32 [5, 640, 640], P(None, 'dp', 'fsdp'), may hold values from -0.109375 to 0.109375
- w_out: float32 [640, 1280], P('dp', 'fsdp'), may hold values from -0.3125 to 0.3125
- norm_params: float32 [8, 640], P('dp', 'fsdp'), may hold values from -0.75 to 1.6
- mean_w_in: float32 [1280, 640], P('dp', 'fsdp'), may hold values from -768 to 768
- mean_w_conv: float32 [5, 640, 640], P(None, 'dp', 'fsdp'), may hold values from -768 to 768
- mean_w_out: float32 [640, 1280], P('dp', 'fsdp'), may hold values from -768 to 768
- mean_norms: float32 [8, 640], P('dp', 'fsdp'), may hold values from -768 to 768
- square_w_in: float32 [1280, 640], P('dp', 'fsdp'), may hold values from 10922.667 to 43690.668
- square_w_conv: float32 [5, 640, 640], P(None, 'dp', 'fsdp'), may hold values from 10922.667 to 43690.668
- square_w_out: float32 [640, 1280], P('dp', 'fsdp'), may hold values from 10922.667 to 43690.668
- square_norms: float32 [8, 640], P('dp', 'fsdp'), may hold values from 10922.667 to 43690.668
Outputs:
- mixed: bfloat16 [65536, 1280], P(('dp', 'fsdp'))
- grad_tokens: bfloat16 [65536, 1280], P(('dp', 'fsdp'))
- type_counts: int32 [25], replicated
- new_w_in: float32 [1280, 640], P('dp', 'fsdp')
- new_w_conv: float32 [5, 640, 640], P(None, 'dp', 'fsdp')
- new_w_out: float32 [640, 1280], P('dp', 'fsdp')
- new_norms: float32 [8, 640], P('dp', 'fsdp')
- new_mean_w_in: float32 [1280, 640], P('dp', 'fsdp')
- new_mean_w_conv: float32 [5, 640, 640], P(None, 'dp', 'fsdp')
- new_mean_w_out: float32 [640, 1280], P('dp', 'fsdp')
- new_mean_norms: float32 [8, 640], P('dp', 'fsdp')
- new_square_w_in: float32 [1280, 640], P('dp', 'fsdp')
- new_square_w_conv: float32 [5, 640, 640], P(None, 'dp', 'fsdp')
- new_square_w_out: float32 [640, 1280], P('dp', 'fsdp')
- new_square_norms: float32 [8, 640], P('dp', 'fsdp')
Inputs may be any that keep to these rules, and one draw needn't show every extreme that they name: `lengths`: each device holds 2 sequences; the last sequence group's first sequence fills its bucket.
All inputs are finite; a program needn't handle non-finite values.
Results may differ from a plain program's by a relative error of at most 0.018.
Values may be sent and summed in bfloat16 or wider, within the bound.
A program may use at most 192 MiB of HBM per device.

v0:
```python
import jax
import jax.numpy as jnp
from jax import lax
from jax.sharding import PartitionSpec as P

D = 1280
INNER = 640
KERNEL_TAPS = 5
DILATION_STRIDE = 8
TYPES = 25
STEP = 5


EPSILON = 1e-05


def normalize(value, gain, bias):
    center = value - jnp.mean(value, axis=-1, keepdims=True)
    spread = jnp.mean(center * center, axis=-1, keepdims=True)
    return center * lax.rsqrt(spread + EPSILON) * gain + bias


def activate(value):
    return jax.nn.gelu(value, approximate=True)


def norm_piece(value, gain, bias):
    return activate(normalize(value, gain, bias))


def gather_params(first, second, third, fourth):
    part = (
        lax.all_gather(first, "fsdp", axis=1, tiled=True),
        lax.all_gather(second, "fsdp", axis=2, tiled=True),
        lax.all_gather(third, "fsdp", axis=1, tiled=True),
        lax.all_gather(fourth, "fsdp", axis=1, tiled=True),
    )
    return (
        lax.all_gather(part[0], "dp", axis=0, tiled=True),
        lax.all_gather(part[1], "dp", axis=1, tiled=True),
        lax.all_gather(part[2], "dp", axis=0, tiled=True),
        lax.all_gather(part[3], "dp", axis=0, tiled=True),
    )


def reduce_grads(first, second, third, fourth):
    part = (
        lax.psum_scatter(first, "fsdp", scatter_dimension=1, tiled=True),
        lax.psum_scatter(second, "fsdp", scatter_dimension=2, tiled=True),
        lax.psum_scatter(third, "fsdp", scatter_dimension=1, tiled=True),
        lax.psum_scatter(fourth, "fsdp", scatter_dimension=1, tiled=True),
    )
    return (
        lax.psum_scatter(
            part[0].astype(jnp.bfloat16), "dp", scatter_dimension=0, tiled=True
        ).astype(jnp.float32),
        lax.psum_scatter(
            part[1].astype(jnp.bfloat16), "dp", scatter_dimension=1, tiled=True
        ).astype(jnp.float32),
        lax.psum_scatter(
            part[2].astype(jnp.bfloat16), "dp", scatter_dimension=0, tiled=True
        ).astype(jnp.float32),
        lax.psum_scatter(
            part[3].astype(jnp.bfloat16), "dp", scatter_dimension=0, tiled=True
        ).astype(jnp.float32),
    )


def stack_taps(value_rows):
    sequence_rows = value_rows.shape[1]
    half_width = KERNEL_TAPS // 2
    padded_input = jnp.pad(
        value_rows, ((0, 0), (half_width * DILATION_STRIDE, half_width * DILATION_STRIDE), (0, 0))
    )
    return jnp.concatenate(
        [
            padded_input[
                :, tap_index * DILATION_STRIDE : tap_index * DILATION_STRIDE + sequence_rows
            ]
            for tap_index in range(KERNEL_TAPS)
        ],
        axis=-1,
    )


def unstack_taps(gradient_tree, sequence_rows):
    half_width = KERNEL_TAPS // 2
    padded_input = jnp.pad(
        gradient_tree,
        ((0, 0), (half_width * DILATION_STRIDE, half_width * DILATION_STRIDE), (0, 0), (0, 0)),
    )
    total_count = padded_input[
        :, 2 * half_width * DILATION_STRIDE : 2 * half_width * DILATION_STRIDE + sequence_rows, 0
    ]
    for tap_index in range(1, KERNEL_TAPS):
        start_offset = (2 * half_width - tap_index) * DILATION_STRIDE
        total_count = (
            total_count + padded_input[:, start_offset : start_offset + sequence_rows, tap_index]
        )
    return total_count


def adamw(master, mean_old, square_old, grad, rate, decay):
    mean_new = 0.5 * mean_old + 0.5 * grad
    square_new = 0.6 * square_old + 0.4 * grad * grad
    mean_hat = mean_new / (1.0 - 0.5**STEP)
    square_hat = square_new / (1.0 - 0.6**STEP)
    weight = master - rate * (mean_hat / (jnp.sqrt(square_hat) + 1e-08) + decay * master)
    return (weight, mean_new, square_new)


def contract_rows(left, right):
    return lax.dot_general(
        left, right, (((0,), (0,)), ((), ())), preferred_element_type=jnp.float32
    )


def contract_cols(left, right):
    return lax.dot_general(
        left, right, (((1,), (1,)), ((), ())), preferred_element_type=jnp.float32
    )


def body(
    tokens,
    cotangent,
    lengths,
    labels,
    w_in,
    w_conv,
    w_out,
    norm_params,
    mean_w_in,
    mean_w_conv,
    mean_w_out,
    mean_norms,
    square_w_in,
    square_w_conv,
    square_w_out,
    square_norms,
):
    slots = lengths.shape[0]
    rows = tokens.shape[0]
    sequence_rows = rows // slots
    places = lax.broadcasted_iota(jnp.int32, (slots, sequence_rows), 1)
    valid = (places < lengths[:, None]).reshape(rows, 1)
    keep = valid.astype(jnp.float32)
    full_in, full_conv, full_out, full_norms = gather_params(
        w_in.astype(jnp.bfloat16),
        w_conv.astype(jnp.bfloat16),
        w_out.astype(jnp.bfloat16),
        norm_params.astype(jnp.bfloat16),
    )
    inner = full_in.shape[1]
    norms = full_norms.astype(jnp.float32)
    gain_a = norms[0:2].reshape(2 * inner)
    bias_a = norms[2:4].reshape(2 * inner)
    source = tokens.astype(jnp.float32)

    def masked_piece(value, gain, bias):
        return norm_piece(value, gain, bias) * keep

    act_a, back_a = jax.vjp(norm_piece, source, gain_a, bias_a)
    low_a = act_a.astype(jnp.bfloat16)
    hid_a = jnp.dot(low_a, full_in, preferred_element_type=jnp.float32)
    middle_activation, back_b = jax.vjp(masked_piece, hid_a, norms[4], norms[5])
    low_b = middle_activation.astype(jnp.bfloat16).reshape(slots, sequence_rows, inner)
    tap_weights = stack_taps(low_b).reshape(rows, KERNEL_TAPS * inner)
    conv_flat = full_conv.reshape(KERNEL_TAPS * inner, inner)
    middle_hidden = jnp.dot(tap_weights, conv_flat, preferred_element_type=jnp.float32)
    act_c, back_c = jax.vjp(norm_piece, middle_hidden, norms[6], norms[7])
    low_c = act_c.astype(jnp.bfloat16)
    hid_c = jnp.dot(low_c, full_out, preferred_element_type=jnp.float32)
    mixed = (source + keep * hid_c).astype(jnp.bfloat16)
    upstream = cotangent.astype(jnp.float32)
    grad_c = (keep * upstream).astype(jnp.bfloat16)
    grad_out = contract_rows(low_c, grad_c)
    d_act_c = contract_cols(grad_c, full_out)
    d_hid_b, d_gain_c, d_bias_c = back_c(d_act_c)
    grad_b = d_hid_b.astype(jnp.bfloat16)
    grad_conv = contract_rows(tap_weights, grad_b).reshape(KERNEL_TAPS, inner, inner)
    d_taps = contract_cols(grad_b, conv_flat)
    d_act_b = unstack_taps(
        d_taps.reshape(slots, sequence_rows, KERNEL_TAPS, inner), sequence_rows
    ).reshape(rows, inner)
    d_hid_a, d_gain_b, d_bias_b = back_b(d_act_b)
    grad_a = d_hid_a.astype(jnp.bfloat16)
    grad_in = contract_rows(low_a, grad_a)
    d_act_a = contract_cols(grad_a, full_in)
    d_source, d_gain_a, d_bias_a = back_a(d_act_a)
    grad_tokens = (upstream + d_source).astype(jnp.bfloat16)
    grad_norms = jnp.concatenate(
        [
            d_gain_a.reshape(2, inner),
            d_bias_a.reshape(2, inner),
            d_gain_b[None],
            d_bias_b[None],
            d_gain_c[None],
            d_bias_c[None],
        ],
        axis=0,
    )
    sum_in, sum_conv, sum_out, sum_norms = reduce_grads(grad_in, grad_conv, grad_out, grad_norms)
    kinds = lax.broadcasted_iota(jnp.int32, (1, TYPES), 1)
    hits = (labels[:, None] == kinds) & valid
    local_counts = jnp.sum(hits.astype(jnp.int32), axis=0)
    type_counts = lax.psum(local_counts, ("dp", "fsdp"))
    new_in = adamw(w_in, mean_w_in, square_w_in, sum_in, 0.5 * D ** (-0.5), 0.01)
    new_conv = adamw(
        w_conv, mean_w_conv, square_w_conv, sum_conv, 0.5 * (KERNEL_TAPS * INNER) ** (-0.5), 0.01
    )
    new_out = adamw(w_out, mean_w_out, square_w_out, sum_out, 0.5 * (INNER // 2) ** (-0.5), 0.01)
    new_norm = adamw(norm_params, mean_norms, square_norms, sum_norms, 0.3, 0.0)
    return (
        mixed,
        grad_tokens,
        type_counts,
        new_in[0],
        new_conv[0],
        new_out[0],
        new_norm[0],
        new_in[1],
        new_conv[1],
        new_out[1],
        new_norm[1],
        new_in[2],
        new_conv[2],
        new_out[2],
        new_norm[2],
    )


def solution(mesh):
    return jax.shard_map(
        body,
        mesh=mesh,
        in_specs=(
            P(("dp", "fsdp"), None),
            P(("dp", "fsdp"), None),
            P(("dp", "fsdp")),
            P(("dp", "fsdp")),
            P("dp", "fsdp"),
            P(None, "dp", "fsdp"),
            P("dp", "fsdp"),
            P("dp", "fsdp"),
            P("dp", "fsdp"),
            P(None, "dp", "fsdp"),
            P("dp", "fsdp"),
            P("dp", "fsdp"),
            P("dp", "fsdp"),
            P(None, "dp", "fsdp"),
            P("dp", "fsdp"),
            P("dp", "fsdp"),
        ),
        out_specs=(
            P(("dp", "fsdp"), None),
            P(("dp", "fsdp"), None),
            P(),
            P("dp", "fsdp"),
            P(None, "dp", "fsdp"),
            P("dp", "fsdp"),
            P("dp", "fsdp"),
            P("dp", "fsdp"),
            P(None, "dp", "fsdp"),
            P("dp", "fsdp"),
            P("dp", "fsdp"),
            P("dp", "fsdp"),
            P(None, "dp", "fsdp"),
            P("dp", "fsdp"),
            P("dp", "fsdp"),
        ),
        check_vma=False,
    )
```

profile of v0, /device:TPU:0, one launch (start us, length us, event | category | flops | bytes accessed | tf_op | source)
XLA Modules:
  0.0 554.6 jit_solution(11055005792385660552)
XLA Ops:
  8.2 11.3 %all_gather.26 = bf16[320,640]{0,1:T(8,128)(2,1)S(1)} all-gather(bf16[320,80]{0,1:T(8,128)(2,1)S(1)} %convert_element_type.89), channel_id=1, replica_groups=mesh['dp'=4,'fsdp'=8] {'fsdp'}, dimensions={1}, use_global_device_ids=true | all-gather | bytes 460800 | tf_op jit(solution)/shard_map/all_gather | solution.py:33
  21.8 17.7 %all_gather.28 = bf16[5,160,640]{1,0,2:T(8,128)(2,1)S(1)} all-gather(bf16[5,160,80]{1,0,2:T(8,128)(2,1)S(1)} %copy.131), channel_id=1, replica_groups=mesh['dp'=4,'fsdp'=8] {'fsdp'}, dimensions={2}, use_global_device_ids=true | all-gather | bytes 1152000 | tf_op jit(solution)/shard_map/all_gather | solution.py:34
  50.3 13.2 %all-gather.1 = bf16[4,2,640]{2,1,0:T(2,128)(2,1)S(1)} all-gather(bf16[1,2,640]{2,1,0:T(2,128)(2,1)S(1)} %bitcast.68), channel_id=1, replica_groups=mesh['dp'=4,'fsdp'=8] {'dp'}, dimensions={0}, use_global_device_ids=true | all-gather | bytes 12800 | tf_op jit(solution)/shard_map/all_gather | solution.py:42
  72.7 8.5 %fusion.12 = bf16[2048,1280]{1,0:T(8,128)(2,1)} fusion(bf16[2048,1280]{1,0:T(8,128)(2,1)} %param.16, f32[1280]{0:T(1024)S(1)} %add.196, f32[1280]{0:T(1024)S(1)} %mul.445, f32[2048]{0:T(1024)S(1)} %fusion.57, f32[2048]{0:T(1024)S(1)} %broadcast_multiply_fusion.2), kind=kLoop, calls=%fused_computation.24 | loop fusion | flops 36700160 | bytes 10512384 | tf_op jit(solution)/shard_map/convert_element_type | solution.py:164
  104.2 34.6 %all-gather.8.cloned.1.call-done = bf16[5,640,640]{2,1,0:T(8,128)(2,1)} async-done(((bf16[5,160,640]{2,1,0:T(8,128)(2,1)}), bf16[5,640,640]{2,1,0:T(8,128)(2,1)}) %all-gather.8.cloned.1.call-update) | async-done | bytes 4096016 | tf_op jit(solution)/shard_map/all_gather | solution.py:40
  138.8 15.5 %fusion.72 = (f32[2048]{0:T(1024)S(1)}, f32[2048,640]{1,0:T(8,128)S(1)}) fusion(bf16[2048,3200]{1,0:T(8,128)(2,1)} %constant_dynamic-update-slice_fusion, bf16[3200,640]{1,0:T(8,128)(2,1)} %bitcast.69), kind=kOutput, calls=%fused_computation.138 | convolution fusion | flops 8389916672 | bytes 22454272 | tf_op jit(solution)/shard_map/dot_general | solution.py:170
  164.0 45.5 %reduce-scatter.20.cloned.1.call-done = f32[640,160]{0,1:T(8,128)} async-done(((f32[640,1280]{0,1:T(8,128)}), f32[640,160]{0,1:T(8,128)}) %reduce-scatter.20.cloned.1.call-update) | async-done | bytes 409616 | tf_op jit(solution)/shard_map/reduce_scatter | solution.py:50
  211.9 20.4 %reduce-scatter.26.cloned.1.call-done = bf16[160,160]{1,0:T(8,128)(2,1)} async-done(((bf16[640,160]{1,0:T(8,128)(2,1)}), bf16[160,160]{1,0:T(8,128)(2,1)}) %reduce-scatter.26.cloned.1.call-update) | async-done | bytes 51216
  233.4 10.2 %all_gather.30 = bf16[160,1280]{0,1:T(8,128)(2,1)S(1)} all-gather(bf16[160,160]{0,1:T(8,128)(2,1)S(1)} %get-tuple-element.139), channel_id=1, replica_groups=mesh['dp'=4,'fsdp'=8] {'fsdp'}, dimensions={1}, use_global_device_ids=true | all-gather | bytes 460800 | tf_op jit(solution)/shard_map/all_gather | solution.py:35
  244.7 35.7 %all-gather.10.cloned.1.call-done = bf16[640,1280]{1,0:T(8,128)(2,1)} async-done(((bf16[160,1280]{1,0:T(8,128)(2,1)}), bf16[640,1280]{1,0:T(8,128)(2,1)}) %all-gather.10.cloned.1.call-update) | async-done | bytes 1638416 | tf_op jit(solution)/shard_map/all_gather | solution.py:41
  280.3 12.2 %multiply_reduce_fusion = (f32[640]{0:T(1024)}, f32[2048]{0:T(1024)S(1)}, f32[640]{0:T(1024)}, f32[2048,640]{1,0:T(8,128)S(1)}) fusion(f32[2048,640]{1,0:T(8,128)} %copy-done.1, f32[2048]{0:T(1024)S(1)} %fusion.59, f32[2048]{0:T(1024)S(1)} %broadcast_multiply_fusion, f32[640]{0:T(1024)S(1)} %get-tuple-element.115, f32[640]{0:T(1024)S(1)} %get-tuple-element.118, ...), kind=kOutput, calls=%fused_computation.59 | convolution fusion | flops 3401315328 | bytes 17410048 | tf_op jit(solution)/shard_map/dot_general | solution.py:119
  298.6 14.0 %fusion.40 = f32[2,1024,5,640]{3,1,2,0:T(8,128)} fusion(bf16[2,1024,640,1]{2,1,3,0:T(8,128)(2,1)S(1)} %bitcast.64, bf16[5,640,640]{2,1,0:T(8,128)(2,1)S(1)} %copy-done.43), kind=kOutput, calls=%fused_computation.71 | convolution fusion | flops 8388608000 | bytes 32931840 | tf_op jit(solution)/shard_map/dot_general | solution.py:119
  312.7 9.0 %fusion.39 = f32[2,1024,1,640]{3,1,2,0:T(8,128)S(1)} fusion(f32[2,1024,5,640]{3,1,2,0:T(8,128)} %fusion.40), kind=kLoop, calls=%fused_computation.57 | loop fusion | flops 5242880 | bytes 36700160 | tf_op jit(solution)/shard_map/add | solution.py:98
  339.4 18.6 %copy.135 = bf16[3200,2048]{1,0:T(8,128)(2,1)} copy(bf16[3200,2048]{0,1:T(8,128)(2,1)} %bitcast.15) | data formatting | bytes 26214400 | tf_op jit(solution)/shard_map/dot_general | solution.py:113
  358.1 15.0 %fusion.42 = f32[5,640,640]{1,2,0:T(8,128)} fusion(bf16[5,640,2048]{2,1,0:T(8,128)(2,1)} %bitcast.53, bf16[2048,640]{1,0:T(8,128)(2,1)S(1)} %add_convert_fusion.1), kind=kOutput, calls=%fused_computation.73 | convolution fusion | flops 8388608000 | bytes 23920640 | tf_op jit(solution)/shard_map/dot_general | solution.py:113
  373.9 39.0 %psum.7 = s32[25]{0:T(128)} all-reduce(s32[25]{0:T(128)S(1)} %convert_reduce_fusion.1), channel_id=1, replica_groups=mesh['dp'=4,'fsdp'=8] {'dp','fsdp'}, use_global_device_ids=true, to_apply=%region_13.14 | all-reduce | flops 25 | bytes 200 | tf_op jit(solution)/shard_map/psum | solution.py:207
  417.3 16.9 %fusion.64 = (f32[1280]{0:T(1024)S(1)}, f32[2048]{0:T(1024)S(1)}, f32[2048,1280]{1,0:T(8,128)}) fusion(f32[1280]{0:T(1024)S(1)} %copy-done.15, f32[2048]{0:T(1024)S(1)} %copy-done.8, bf16[2048,1280]{1,0:T(8,128)(2,1)} %param.16, f32[1280]{0:T(1024)S(1)} %copy-done.25, f32[2048]{0:T(1024)S(1)} %copy-done.13, ...), kind=kOutput, calls=%fused_computation.133 | convolution fusion | flops 3431461632 | bytes 22658048 | tf_op jit(solution)/shard_map/dot_general | solution.py:119
  434.3 7.9 %fusion.15 = (f32[1280]{0:T(1024)S(1)}, f32[2048]{0:T(1024)S(1)}) fusion(f32[2048,1280]{1,0:T(8,128)} %get-tuple-element.148, bf16[2048,1280]{1,0:T(8,128)(2,1)} %param.16, f32[2048]{0:T(1024)S(1)} %copy-done.13, f32[2048]{0:T(1024)S(1)} %copy-done.8, f32[2048]{0:T(1024)S(1)} %multiply_multiply_fusion.9, f32[1280]{0:T(1024)S(1)} %copy-done.15), kind=kLoop, calls=%fused_computation.27 | loop fusion | flops 28832512 | bytes 15771648 | tf_op jit(solution)/shard_map/transpose(jvp())/reduce_sum | solution.py:20
  445.3 11.5 %fusion.17 = bf16[2048,1280]{1,0:T(8,128)(2,1)} fusion(bf16[2048,1280]{1,0:T(8,128)(2,1)} %param.17, f32[2048]{0:T(1024)S(1)} %negate_multiply_fusion, f32[2048]{0:T(1024)S(1)} %multiply_multiply_fusion.9, f32[2048]{0:T(1024)S(1)} %copy-done.8, bf16[2048,1280]{1,0:T(8,128)(2,1)} %param.16, f32[2048]{0:T(1024)S(1)} %copy-done.13, ...), kind=kLoop, calls=%fused_computation.29 | loop fusion | flops 28835840 | bytes 26252288 | tf_op jit(solution)/shard_map/convert_element_type | solution.py:191
  463.6 10.8 %fusion.23 = bf16[2048,1280]{1,0:T(8,128)(2,1)} fusion(bf16[2048,1280]{1,0:T(8,128)(2,1)} %param.16, bf16[640,1280]{1,0:T(8,128)(2,1)} %all-gather.10.cloned.1.call-done, f32[2048]{0:T(1024)S(1)} %convert_element_type.85, f32[2048,640]{1,0:T(8,128)} %copy-done.1, f32[640]{0:T(1024)S(1)} %copy-done.37, f32[640]{0:T(1024)S(1)} %copy-done.30, ...), kind=kOutput, calls=%fused_computation.35 | convolution fusion | flops 3382968320 | bytes 17396736 | tf_op jit(solution)/shard_map/dot_general | solution.py:173
  474.5 22.6 %reduce-scatter.28.cloned.1.call-done = f32[80,8]{1,0:T(8,128)} async-done(((f32[640,8]{1,0:T(8,128)}), f32[80,8]{1,0:T(8,128)}) %reduce-scatter.28.cloned.1.call-update) | async-done | bytes 2576
  497.9 11.8 %all-reduce.2 = bf16[8,80]{1,0:T(8,128)(2,1)S(1)} all-reduce(bf16[8,80]{1,0:T(8,128)(2,1)S(1)} %copy.161), channel_id=9, replica_groups=mesh['dp'=4,'fsdp'=8] {'dp'}, use_global_device_ids=true, to_apply=%region_27.28.clone | all-reduce | flops 640 | bytes 2560
  510.3 9.7 %reduce-scatter.22.cloned.1.call-done = bf16[320,80]{1,0:T(8,128)(2,1)} async-done(((bf16[1280,80]{1,0:T(8,128)(2,1)}), bf16[320,80]{1,0:T(8,128)(2,1)}) %reduce-scatter.22.cloned.1.call-update) | async-done | bytes 51216
  521.9 20.8 %reduce-scatter.24.cloned.1.call-done = bf16[160,400]{1,0:T(8,128)(2,1)} async-done(((bf16[640,400]{1,0:T(8,128)(2,1)}), bf16[160,400]{1,0:T(8,128)(2,1)}) %reduce-scatter.24.cloned.1.call-update) | async-done | bytes 128016
  (214 shorter events, 105.8 us)
Async XLA Ops:
  7.2 74.1 %all-gather.6.cloned.1.call-start = ((), (), s32[]{:S(2)}) async-start(), calls=%async_computation.7 | async-start | bytes 2048000 | tf_op jit(solution)/shard_map/all_gather | solution.py:39
  8.2 55.3 %copy-start.42 = (s32[2]{0:T(128)S(1)}, s32[2]{0:T(128)}, u32[]{:S(2)}) copy-start(s32[2]{0:T(128)} %param.18) | copy-start | bytes 28
  20.5 118.3 %all-gather.8.cloned.1.call-start = ((), (), s32[]{:S(2)}) async-start(), calls=%async_computation.8 | async-start | bytes 5120000 | tf_op jit(solution)/shard_map/all_gather | solution.py:40
  42.3 167.2 %reduce-scatter.20.cloned.1.call-start = ((), (), s32[]{:S(2)}) async-start(), calls=%async_computation.12 | async-start | bytes 3686400 | tf_op jit(solution)/shard_map/reduce_scatter | solution.py:50
  72.7 207.6 %copy-start.36 = (f32[640]{0:T(1024)}, f32[640]{0:T(1024)S(1)}, u32[]{:S(2)}) copy-start(f32[640]{0:T(1024)S(1)} %get-tuple-element.118) | copy-start | bytes 7684
  72.7 219.9 %copy-start.29 = (f32[640]{0:T(1024)}, f32[640]{0:T(1024)S(1)}, u32[]{:S(2)}) copy-start(f32[640]{0:T(1024)S(1)} %get-tuple-element.115) | copy-start | bytes 7684
  154.4 138.2 %copy-start.18 = (f32[2048]{0:T(1024)}, f32[2048]{0:T(1024)S(1)}, u32[]{:S(2)}) copy-start(f32[2048]{0:T(1024)S(1)} %broadcast_multiply_fusion) | copy-start | bytes 24580
  155.1 137.5 %copy-start.22 = (f32[2048]{0:T(1024)}, f32[2048]{0:T(1024)S(1)}, u32[]{:S(2)}) copy-start(f32[2048]{0:T(1024)S(1)} %fusion.59) | copy-start | bytes 24580
  156.7 54.9 %copy-start.9 = (f32[160,160]{1,0:T(8,128)S(1)}, f32[160,160]{1,0:T(8,128)}, u32[]{:S(2)}) copy-start(f32[160,160]{1,0:T(8,128)} %param.22) | copy-start | bytes 307204
  156.7 55.0 %copy-start.10 = (f32[160,160]{1,0:T(8,128)S(1)}, f32[160,160]{1,0:T(8,128)}, u32[]{:S(2)}) copy-start(f32[160,160]{1,0:T(8,128)} %param.26) | copy-start | bytes 307204
  164.0 47.8 %copy-start.11 = (f32[160,160]{1,0:T(8,128)S(1)}, f32[160,160]{1,0:T(8,128)}, u32[]{:S(2)}) copy-start(f32[160,160]{1,0:T(8,128)} %param.30) | copy-start | bytes 307204
  164.0 68.3 %reduce-scatter.26.cloned.1.call-start = ((), (), s32[]{:S(2)}) async-start(), calls=%async_computation.15 | async-start | bytes 409600
  211.5 68.8 %all-gather.10.cloned.1.call-start = ((), (), s32[]{:S(2)}) async-start(), calls=%async_computation.9 | async-start | bytes 2048000 | tf_op jit(solution)/shard_map/all_gather | solution.py:41
  244.6 198.7 %reduce-scatter.16.cloned.1.call-start = ((), (), s32[]{:S(2)}) async-start(), calls=%async_computation.10 | async-start | bytes 3686400 | tf_op jit(solution)/shard_map/reduce_scatter | solution.py:48
  339.4 120.1 %reduce-scatter.18.cloned.1.call-start = ((), (), s32[]{:S(2)}) async-start(), calls=%async_computation.11 | async-start | bytes 9216000 | tf_op jit(solution)/shard_map/reduce_scatter | solution.py:49
  373.2 123.9 %reduce-scatter.28.cloned.1.call-start = ((), (), s32[]{:S(2)}) async-start(), calls=%async_computation.16 | async-start | bytes 368640
  443.2 76.9 %reduce-scatter.22.cloned.1.call-start = ((), (), s32[]{:S(2)}) async-start(), calls=%async_computation.13 | async-start | bytes 409600
  445.2 97.5 %reduce-scatter.24.cloned.1.call-start = ((), (), s32[]{:S(2)}) async-start(), calls=%async_computation.14 | async-start | bytes 819200
  463.6 46.2 %copy-start.39 = (f32[2,80]{1,0:T(2,128)S(1)}, f32[2,80]{1,0:T(2,128)}, u32[]{:S(2)}) copy-start(f32[2,80]{1,0:T(2,128)} %param.23) | copy-start | bytes 1924
  463.6 46.2 %copy-start.40 = (f32[2,80]{1,0:T(2,128)S(1)}, f32[2,80]{1,0:T(2,128)}, u32[]{:S(2)}) copy-start(f32[2,80]{1,0:T(2,128)} %param.27) | copy-start | bytes 1924
  463.6 46.2 %copy-start.41 = (f32[2,80]{1,0:T(2,128)S(1)}, f32[2,80]{1,0:T(2,128)}, u32[]{:S(2)}) copy-start(f32[2,80]{1,0:T(2,128)} %param.31) | copy-start | bytes 1924
  463.6 57.5 %copy-start.4 = (f32[320,80]{0,1:T(8,128)S(1)}, f32[320,80]{0,1:T(8,128)}, u32[]{:S(2)}) copy-start(f32[320,80]{0,1:T(8,128)} %param.20) | copy-start | bytes 307204
  463.6 57.5 %copy-start.16 = (f32[320,80]{0,1:T(8,128)S(1)}, f32[320,80]{0,1:T(8,128)}, u32[]{:S(2)}) copy-start(f32[320,80]{0,1:T(8,128)} %param.24) | copy-start | bytes 307204
  463.6 57.5 %copy-start.17 = (f32[320,80]{0,1:T(8,128)S(1)}, f32[320,80]{0,1:T(8,128)}, u32[]{:S(2)}) copy-start(f32[320,80]{0,1:T(8,128)} %param.28) | copy-start | bytes 307204
  (37 other events, 757.6 us)
Sparse Core Ops, SparseCore 0:
  20.6 38.5 all-gather.5
  60.7 78.0 all-gather.7
  164.1 45.3 reduce-scatter.19
  212.2 20.0 reduce-scatter.25
  244.7 35.5 all-gather.9
  339.5 46.0 reduce-scatter.15
  389.3 70.1 reduce-scatter.17
  463.3 33.7 reduce-scatter.27
  500.1 19.9 reduce-scatter.21
  522.3 20.3 reduce-scatter.23
where the time goes:
time: 560 us; the launch traced here: 555 us
  waiting for transfers between devices  192 us (34%)
  blocking collectives  111 us (20%)
  matrix products  105 us (19%)
  other arithmetic  74.4 us (13%)
  local copies, waits for them, and re-layouts  56 us (10%)
  between operations  16.2 us (3%)
    unnamed x14, waiting for transfers between devices  73.7 us
    reduce_scatter x1, waiting for transfers between devices, reduce_grads(): lax.psum_scatter(third, 'fsdp', scatter_dimension=1, tiled=True)  45.5 us
    dot_general x3, matrix products, contract_cols(): lax.dot_general(left, right, (((1,), (1,)), ((), ())), preferred_element_...  43.2 us
    psum x1, blocking collectives, body(): type_counts = lax.psum(local_counts, ('dp', 'fsdp'))  39 us
    all_gather x1, waiting for transfers between devices, gather_params(): lax.all_gather(part[2], 'dp', axis=0, tiled=True)  35.7 us
    all_gather x1, waiting for transfers between devices, gather_params(): lax.all_gather(part[1], 'dp', axis=1, tiled=True)  34.6 us
    unnamed x129, local copies, waits for them, and re-layouts  29.4 us
    dot_general x3, matrix products, contract_rows(): lax.dot_general(left, right, (((0,), (0,)), ((), ())), preferred_element_...  28 us
  transfers between devices with their start and end apart: 10, of which 8 were waited for; matrix products, arithmetic and copies ran while one was open for 25% of the time, Pallas kernels for 0%

commit v1 on v0

--- a/solution.py
+++ b/solution.py
@@ -1,6 +1,11 @@
+import functools
+from types import SimpleNamespace
+
 import jax
 import jax.numpy as jnp
 from jax import lax
+from jax.experimental import pallas as pl
+from jax.experimental.pallas import tpu as pltpu
 from jax.sharding import PartitionSpec as P
 
 D = 1280
@@ -14,7 +19,7 @@
 EPSILON = 1e-05
 
 
-def normalize(value, gain, bias):
+def plain_normalize(value, gain, bias):
     center = value - jnp.mean(value, axis=-1, keepdims=True)
     spread = jnp.mean(center * center, axis=-1, keepdims=True)
     return center * lax.rsqrt(spread + EPSILON) * gain + bias
@@ -25,7 +30,7 @@
 
 
 def norm_piece(value, gain, bias):
-    return activate(normalize(value, gain, bias))
+    return activate(plain_normalize(value, gain, bias))
 
 
 def gather_params(first, second, third, fourth):
@@ -121,7 +126,7 @@
     )
 
 
-def body(
+def plain_body(
     tokens,
     cotangent,
     lengths,
@@ -230,9 +235,1011 @@
     )
 
 
+F32, BF16 = jnp.float32, jnp.bfloat16
+MESH = pl.DeviceIdType.MESH
+DP_RANKS, PLANE = 4, 8
+HALO = (KERNEL_TAPS // 2) * DILATION_STRIDE
+GELU_SCALE, GELU_CUBE = 0.7978845608, 0.044715
+BLOCK = 256
+CONV_LANES = 256
+NAMES = ("in", "conv", "out")
+
+
+def dot_nn(a, b):
+    return lax.dot_general(a, b, (((1,), (0,)), ((), ())), preferred_element_type=F32)
+
+
+def dot_nt(a, b):
+    return lax.dot_general(a, b, (((1,), (1,)), ((), ())), preferred_element_type=F32)
+
+
+def dot_tn(a, b):
+    return lax.dot_general(a, b, (((0,), (0,)), ((), ())), preferred_element_type=F32)
+
+
+def gelu(z):
+    t = jnp.tanh(z * (GELU_SCALE + (GELU_SCALE * GELU_CUBE) * (z * z)))
+    h = 0.5 * z
+    return h + h * t
+
+
+def gelu_grad(z):
+    zz = z * z
+    t = jnp.tanh(z * (GELU_SCALE + (GELU_SCALE * GELU_CUBE) * zz))
+    slope = z * (GELU_SCALE + (3.0 * GELU_SCALE * GELU_CUBE) * zz)
+    return 0.5 * (1.0 + t + (1.0 - t * t) * slope)
+
+
+def stats(x):
+    c = x - jnp.mean(x, axis=-1, keepdims=True)
+    r = lax.rsqrt(jnp.mean(c * c, axis=-1, keepdims=True) + EPSILON)
+    return c * r, r
+
+
+def loop(n, step, hooks=None):
+    def one(i, carry):
+        step(i)
+        for at, calls in (hooks or {}).items():
+
+            @pl.when(i == at)
+            def _(calls=calls):
+                for call in calls:
+                    call()
+
+        return carry
+
+    lax.fori_loop(0, n, one, 0)
+
+
+def once(step, i):
+    step(i)
+
+
+def block(i, n):
+    return pl.ds(pl.multiple_of(i * n, n), n)
+
+
+def round_up(n, m=128):
+    return -(-n // m) * m
+
+
+class Place:
+    def __init__(self):
+        self.d = lax.axis_index("dp")
+        f = lax.axis_index("fsdp")
+        self.f = f
+        self.c, self.x, self.y = f % 2, (f // 2) % 2, f // 4
+        self.oc, self.ox, self.oy = 1 - self.c, 1 - self.x, 1 - self.y
+        self.ranks = [(self.d + j) % DP_RANKS for j in range(DP_RANKS)]
+        self.sib = {"fsdp": f + 1 - 2 * self.c}
+        self.xn = {"fsdp": f + 2 - 4 * self.x}
+        self.yn = {"fsdp": f + 4 - 8 * self.y}
+        self.zn = [{"dp": p} for p in self.ranks[1:]]
+
+
+def barrier(pc):
+    sem = pltpu.get_barrier_semaphore()
+    peers = [pc.sib, pc.xn, pc.yn] + pc.zn
+    for p in peers:
+        pl.semaphore_signal(sem, inc=1, device_id=p, device_id_type=MESH)
+    pl.semaphore_wait(sem, len(peers))
+
+
+def remote(src, dst, send, recv, device):
+    return pltpu.make_async_remote_copy(
+        src_ref=src, dst_ref=dst, send_sem=send, recv_sem=recv, device_id=device, device_id_type=MESH
+    )
+
+
+def halves(name, shape):
+    h, lanes = shape[-2:]
+    if name == "out":
+        return (slice(0, h // 2), slice(None)), (slice(h // 2, h), slice(None))
+    cut = round_up(lanes // 2)
+    return (slice(None), slice(0, cut)), (slice(None), slice(cut, lanes))
+
+
+class Gather:
+    SEMS = 13
+
+    def __init__(self, pc, name, w, zr, send, recv):
+        self.pc, self.w, self.zr, self.send, self.recv = pc, w, zr, send, recv
+        self.name = name
+        self.cut = halves(name, w.shape)
+        self.sent = []
+
+    def z(self, j):
+        pc = self.pc
+        mine = self.zr.at[pc.d]
+        return remote(mine, mine, self.send.at[j - 1], self.recv.at[pc.d], pc.zn[j - 1])
+
+    def z_in(self, j):
+        pc = self.pc
+        p = pc.ranks[j]
+        return remote(self.zr.at[p], self.zr.at[p], self.send.at[j - 1], self.recv.at[p], pc.zn[j - 1])
+
+    def start(self):
+        for j in (2, 1, 3):
+            self.z(j).start()
+
+    def go(self, ref, i, device):
+        c = remote(ref, ref, self.send.at[i], self.recv.at[i], device)
+        c.start()
+        self.sent.append((i, ref, device))
+
+    def arrived(self, i, ref):
+        remote(ref, ref, self.send.at[i], self.recv.at[i], self.pc.sib).wait_recv()
+
+    def at(self, y, x, c, half=None):
+        r = self.w.at[y, x, c]
+        return r if half is None else r.at[self.cut[half]]
+
+    def own(self):
+        pc = self.pc
+        for j in range(1, DP_RANKS):
+            self.z_in(j).wait_recv()
+        ASSEMBLE[self.name](self.w, self.zr, (pc.y, pc.x, pc.c))
+        mine = self.at(pc.y, pc.x, pc.c)
+        self.go(mine, 4, pc.xn)
+        self.go(mine, 5, pc.yn)
+        self.go(mine, 8, pc.sib)
+
+    def from_x(self):
+        pc = self.pc
+        r = self.at(pc.y, pc.ox, pc.c)
+        self.arrived(4, r)
+        self.go(self.at(pc.y, pc.ox, pc.c, 1), 7, pc.yn)
+        self.go(r, 9, pc.sib)
+
+    def from_y(self):
+        pc = self.pc
+        r = self.at(pc.oy, pc.x, pc.c)
+        self.arrived(5, r)
+        self.go(self.at(pc.oy, pc.x, pc.c, 0), 6, pc.xn)
+        self.go(r, 10, pc.sib)
+
+    def from_diagonal(self):
+        pc = self.pc
+        for half in (0, 1):
+            r = self.at(pc.oy, pc.ox, pc.c, half)
+            self.arrived(6 + half, r)
+            self.go(r, 11 + half, pc.sib)
+
+    def from_sibling(self):
+        pc = self.pc
+        o = pc.oc
+        self.arrived(8, self.at(pc.y, pc.x, o))
+        self.arrived(9, self.at(pc.y, pc.ox, o))
+        self.arrived(10, self.at(pc.oy, pc.x, o))
+        for half in (0, 1):
+            self.arrived(11 + half, self.at(pc.oy, pc.ox, o, half))
+
+    def finish(self):
+        for j in range(1, DP_RANKS):
+            self.z(j).wait_send()
+        for i, ref, device in self.sent:
+            remote(ref, ref, self.send.at[i], self.recv.at[i], device).wait_send()
+
+
+def assemble_in(w, zr, own):
+    n = w.shape[-1] // DP_RANKS
+    w[own] = jnp.concatenate([zr[i][:, :n] for i in range(DP_RANKS)], axis=1)
+
+
+def assemble_conv(w, zr, own):
+    n = w.shape[-1] // (DP_RANKS * KERNEL_TAPS)
+    w[own] = jnp.concatenate(
+        [zr[i][:, k * n : (k + 1) * n] for k in range(KERNEL_TAPS) for i in range(DP_RANKS)], axis=1
+    )
+
+
+def assemble_out(w, zr, own):
+    n = w.shape[-1] // DP_RANKS
+    h = zr.shape[1]
+    for part in range(2):
+        w[own + (slice(part * h, (part + 1) * h),)] = jnp.concatenate(
+            [zr[i][:, part * n : (part + 1) * n] for i in range(DP_RANKS)], axis=1
+        )
+
+
+ASSEMBLE = {"in": assemble_in, "conv": assemble_conv, "out": assemble_out}
+
+
+class Scatter:
+    SEMS = 9
+
+    def __init__(self, pc, name, g, rcv, r1a, r1b, r2a, r2b, zs, zr, send, recv):
+        self.pc, self.name, self.g, self.rcv = pc, name, g, rcv
+        self.r1a, self.r1b, self.r2a, self.r2b = r1a, r1b, r2a, r2b
+        self.zs, self.zr, self.send, self.recv = zs, zr, send, recv
+        self.cut = halves(name, g.shape)
+
+    def copy(self, i, src, dst, device):
+        return remote(src, dst, self.send.at[i], self.recv.at[i], device)
+
+    def half(self, ref, k):
+        return ref.at[(slice(None),) * (len(ref.shape) - 2) + self.cut[k]]
+
+    def c0(self):
+        pc = self.pc
+        return self.copy(0, self.g.at[:, :, pc.oc], self.rcv, pc.sib)
+
+    def a1(self):
+        pc = self.pc
+        return self.copy(1, self.half(self.g.at[:, pc.ox, pc.c], 0), self.r1a, pc.xn)
+
+    def b1(self):
+        pc = self.pc
+        return self.copy(2, self.half(self.g.at[pc.oy, :, pc.c], 1), self.r1b, pc.yn)
+
+    def a2(self):
+        pc = self.pc
+        return self.copy(3, self.half(self.g.at[pc.oy, pc.x, pc.c], 0), self.r2a, pc.yn)
+
+    def b2(self):
+        pc = self.pc
+        return self.copy(4, self.half(self.g.at[pc.y, pc.ox, pc.c], 1), self.r2b, pc.xn)
+
+    def z(self, j):
+        pc = self.pc
+        return remote(
+            self.zs.at[pc.ranks[j]], self.zr.at[pc.d], self.send.at[4 + j], self.recv.at[5 + pc.d], pc.zn[j - 1]
+        )
+
+    def z_in(self, j):
+        pc = self.pc
+        p = pc.ranks[j]
+        return remote(self.zs.at[p], self.zr.at[p], self.send.at[4 + j], self.recv.at[5 + p], pc.zn[j - 1])
+
+    def start(self):
+        self.c0().start()
+
+    def step1(self):
+        pc = self.pc
+        self.c0().wait_recv()
+        for y in range(2):
+            for x in range(2):
+                self.g[y, x, pc.c] = (self.g[y, x, pc.c].astype(F32) + self.rcv[y, x].astype(F32)).astype(BF16)
+        self.a1().start()
+        self.b1().start()
+
+    def add(self, y, x, k, ref):
+        idx = (y, x, self.pc.c) + self.cut[k]
+        self.g[idx] = (self.g[idx].astype(F32) + ref[...].astype(F32)).astype(BF16)
+
+    def step2(self):
+        pc = self.pc
+        self.a1().wait_recv()
+        self.add(pc.oy, pc.x, 0, self.r1a.at[pc.oy])
+        self.a2().start()
+        self.b1().wait_recv()
+        self.add(pc.y, pc.ox, 1, self.r1b.at[pc.ox])
+        self.b2().start()
+        self.add(pc.y, pc.x, 0, self.r1a.at[pc.y])
+        self.add(pc.y, pc.x, 1, self.r1b.at[pc.x])
+
+    def step3(self):
+        pc = self.pc
+        self.a2().wait_recv()
+        self.add(pc.y, pc.x, 0, self.r2a)
+        self.b2().wait_recv()
+        self.add(pc.y, pc.x, 1, self.r2b)
+        SPLIT[self.name](self.zs, self.g[pc.y, pc.x, pc.c])
+        for j in (2, 1, 3):
+            self.z(j).start()
+
+    def step4(self, out):
+        pc = self.pc
+        total = self.zs[pc.d].astype(F32)
+        for j in range(1, DP_RANKS):
+            self.z_in(j).wait_recv()
+            total = total + self.zr[pc.ranks[j]].astype(F32)
+        out[...] = total
+
+    def finish(self):
+        for c in (self.c0(), self.a1(), self.b1(), self.a2(), self.b2()):
+            c.wait_send()
+        for j in range(1, DP_RANKS):
+            self.z(j).wait_send()
+
+
+def split_in(zs, v):
+    n = v.shape[1] // DP_RANKS
+    for i in range(DP_RANKS):
+        zs[i, :, 0:n] = v[:, i * n : (i + 1) * n]
+
+
+def split_conv(zs, v):
+    n = v.shape[1] // (DP_RANKS * KERNEL_TAPS)
+    for i in range(DP_RANKS):
+        starts = [(DP_RANKS * k + i) * n for k in range(KERNEL_TAPS)]
+        zs[i, :, 0 : KERNEL_TAPS * n] = jnp.concatenate([v[:, s : s + n] for s in starts], axis=1)
+
+
+def split_out(zs, v):
+    n = v.shape[1] // DP_RANKS
+    h = zs.shape[1]
+    for i in range(DP_RANKS):
+        zs[i, :, 0 : 2 * n] = jnp.concatenate(
+            [v[0:h, i * n : (i + 1) * n], v[h : 2 * h, i * n : (i + 1) * n]], axis=1
+        )
+
+
+SPLIT = {"in": split_in, "conv": split_conv, "out": split_out}
+
+
+class NormGather:
+    SEMS = 7
+
+    def __init__(self, pc, nz, nw, send, recv):
+        self.pc, self.nz, self.nw, self.send, self.recv = pc, nz, nw, send, recv
+
+    def z(self, j, p):
+        pc = self.pc
+        return remote(self.nz.at[p], self.nz.at[p], self.send.at[j - 1], self.recv.at[p], pc.zn[j - 1])
+
+    def start(self):
+        for j in range(1, DP_RANKS):
+            self.z(j, self.pc.d).start()
+
+    def stage(self, k):
+        pc = self.pc
+        ref = (self.nw.at[pc.y, pc.x, pc.c], self.nw.at[pc.y, pc.x], self.nw.at[pc.y])[k]
+        return remote(ref, ref, self.send.at[3 + k], self.recv.at[4 + k], (pc.sib, pc.xn, pc.yn)[k])
+
+    def stage_in(self, k):
+        pc = self.pc
+        ref = (self.nw.at[pc.y, pc.x, pc.oc], self.nw.at[pc.y, pc.ox], self.nw.at[pc.oy])[k]
+        return remote(ref, ref, self.send.at[3 + k], self.recv.at[4 + k], (pc.sib, pc.xn, pc.yn)[k])
+
+    def own(self):
+        pc = self.pc
+        for j in range(1, DP_RANKS):
+            self.z(j, pc.ranks[j]).wait_recv()
+        self.nw[pc.y, pc.x, pc.c] = jnp.concatenate([self.nz[i][0:2] for i in range(DP_RANKS)], axis=0)
+        self.stage(0).start()
+
+    def next(self, k):
+        self.stage_in(k).wait_recv()
+        if k < 2:
+            self.stage(k + 1).start()
+
+    def whole(self, width):
+        return jnp.concatenate([self.nw[f // 4, (f // 2) % 2, f % 2][:, 0:width] for f in range(PLANE)], axis=1)
+
+    def finish(self):
+        for j in range(1, DP_RANKS):
+            self.z(j, self.pc.d).wait_send()
+        for k in range(3):
+            self.stage(k).wait_send()
+
+
+class SmallSum:
+    SEMS = 7
+
+    def __init__(self, pc, acc, got, zgot, send, recv):
+        self.pc, self.acc, self.got, self.zgot, self.send, self.recv = pc, acc, got, zgot, send, recv
+
+    def stage(self, k):
+        pc = self.pc
+        return remote(
+            self.acc.at[k], self.got.at[k], self.send.at[k], self.recv.at[4 + k], (pc.sib, pc.xn, pc.yn)[k]
+        )
+
+    def z(self, j):
+        pc = self.pc
+        return remote(self.acc.at[3], self.zgot.at[pc.d], self.send.at[2 + j], self.recv.at[pc.d], pc.zn[j - 1])
+
+    def z_in(self, j):
+        pc = self.pc
+        p = pc.ranks[j]
+        return remote(self.acc.at[3], self.zgot.at[p], self.send.at[2 + j], self.recv.at[p], pc.zn[j - 1])
+
+    def start(self):
+        self.stage(0).start()
+
+    def next(self, k):
+        self.stage(k).wait_recv()
+        self.acc[k + 1] = self.acc[k] + self.got[k]
+        if k < 2:
+            self.stage(k + 1).start()
+        else:
+            for j in range(1, DP_RANKS):
+                self.z(j).start()
+
+    def total(self):
+        for j in range(1, DP_RANKS):
+            self.z_in(j).wait_recv()
+        self.zgot[self.pc.d] = self.acc[3]
+        return (self.zgot[0] + self.zgot[1]) + (self.zgot[2] + self.zgot[3])
+
+    def finish(self):
+        for k in range(3):
+            self.stage(k).wait_send()
+        for j in range(1, DP_RANKS):
+            self.z(j).wait_send()
+
+
+def norm_back(n, r, gain, bias, e, sums, row):
+    dz = e * gelu_grad(n * gain + bias)
+    width = n.shape[1]
+    sums[row : row + 1, 0:width] += jnp.sum(dz * n, axis=0, keepdims=True)
+    sums[row + 1 : row + 2, 0:width] += jnp.sum(dz, axis=0, keepdims=True)
+    dn = dz * gain
+    m1 = jnp.mean(dn, axis=-1, keepdims=True)
+    m2 = jnp.mean(dn * n, axis=-1, keepdims=True)
+    return r * (dn - m1 - n * m2)
+
+
+def block_kernel(refs):
+    r = refs
+    pc = Place()
+    tokens, cot_in, lens, labels = r.tokens, r.cot_in, r.lens, r.labels
+    x, cot, act_a, n_b, act_c = r.x, r.cot, r.act_a, r.n_b, r.act_c
+    scale, sums, tail_rows = r.scale, r.sums, r.tail
+    b_even, b_odd, g_even, g_odd, back_t = r.b_even, r.b_odd, r.g_even, r.g_odd, r.back_t
+    rows, width = x.shape
+    inner = n_b.shape[1]
+    slots = lens.shape[0]
+    seq = rows // slots
+    blocks = seq // BLOCK
+    grad_a = act_c
+
+    wide = {"in": r.w_in, "conv": r.w_conv, "out": r.w_out}
+    gather = {n: Gather(pc, n, wide[n], getattr(r, "zg_" + n), getattr(r, "gs_" + n), getattr(r, "gr_" + n)) for n in NAMES}
+    norm_gather = NormGather(pc, r.nz, r.nw, r.ns, r.nr)
+    small = SmallSum(pc, r.sm_acc, r.sm_got, r.sm_z, r.sm_s, r.sm_r)
+
+    load_x = pltpu.make_async_copy(tokens, x, r.io.at[0])
+    load_cot = pltpu.make_async_copy(cot_in, cot, r.io.at[1])
+    load_x.start()
+
+    cols = r.p_in.shape[0]
+    r.nz[pc.d, 0:2, 0:cols] = r.p_norms[...].astype(BF16).astype(F32)
+    barrier(pc)
+    norm_gather.start()
+    r.zg_in[pc.d, :, 0 : r.p_in.shape[1]] = r.p_in[...].astype(BF16)
+    gather["in"].start()
+    depth = r.p_conv.shape[1]
+    for k in range(KERNEL_TAPS):
+        r.zg_conv[pc.d, :, k * depth : (k + 1) * depth] = r.p_conv[k].T.astype(BF16)
+    p_out = r.p_out[...].T.astype(BF16)
+    h_out = r.zg_out.shape[1]
+    r.zg_out[pc.d, :, 0 : 2 * depth] = jnp.concatenate([p_out[0:h_out], p_out[h_out : 2 * h_out]], axis=1)
+
+    sums[...] = jnp.zeros_like(sums)
+    pad = jnp.zeros((HALO, inner), BF16)
+    for s in range(slots):
+        for buf in (b_even, g_even):
+            buf[s, 0:HALO, :] = pad
+            buf[s, seq + HALO : seq + 2 * HALO, :] = pad
+
+    def kept(s, first, count):
+        return first + lax.broadcasted_iota(jnp.int32, (count, 1), 0) < lens[s]
+
+    lab = labels[...]
+    place = (
+        lax.broadcasted_iota(jnp.int32, lab.shape, 0) * lab.shape[1] + lax.broadcasted_iota(jnp.int32, lab.shape, 1)
+    )
+    valid = place < 0
+    for s in range(slots):
+        valid = valid | ((place >= s * seq) & (place < s * seq + lens[s]))
+    lane = lax.broadcasted_iota(jnp.int32, (1, inner), 1)
+    counts = jnp.zeros((1, inner), F32)
+    for c in range(TYPES):
+        hits = jnp.sum(jnp.where(valid & (lab == c), 1.0, 0.0), keepdims=True)
+        counts = counts + jnp.where(lane == c, hits, 0.0)
+
+    load_x.wait()
+    load_cot.start()
+    strip = BLOCK // 2
+
+    def first_stats(i):
+        at = block(i, strip)
+        n, rs = stats(x[at, :].astype(F32))
+        x[at, :] = n.astype(BF16)
+        scale[at, 0:1] = rs
+
+    loop(rows // strip, first_stats)
+    norm_gather.own()
+    gather["in"].own()
+    gather["conv"].start()
+    for k in range(3):
+        norm_gather.next(k)
+    r.norms[...] = norm_gather.whole(cols)
+    norms = r.norms
+    gain_a = jnp.concatenate([norms[0:1, :], norms[1:2, :]], axis=1)
+    bias_a = jnp.concatenate([norms[2:3, :], norms[3:4, :]], axis=1)
+    gain_b, bias_b, gain_c, bias_c = (norms[i : i + 1, :] for i in range(4, 8))
+
+    def first_act(i):
+        at = block(i, strip)
+        act_a[at, :] = gelu(x[at, :].astype(F32) * gain_a + bias_a).astype(BF16)
+
+    half_way = rows // strip // 2
+    loop(half_way, first_act)
+    gather["in"].from_x()
+    gather["in"].from_y()
+    loop(half_way, lambda i: first_act(i + half_way))
+    gather["in"].from_diagonal()
+    gather["conv"].own()
+    gather["out"].start()
+    gather["in"].from_sibling()
+    w_in = r.w_in
+    w_conv = r.w_conv
+    w_out = r.w_out
+
+    def flat(w):
+        v = w[...]
+        return v.reshape(PLANE * v.shape[3], v.shape[4])
+
+    def shifted_store(even, odd, s, i, value):
+        even[s, pl.ds(pl.multiple_of(i * BLOCK + HALO, 16), BLOCK), :] = value.astype(BF16)
+        before = jnp.where(i == 0, 0.0, tail_rows[...])
+        late = value[BLOCK - 8 :]
+        odd[s, block(i, BLOCK), :] = jnp.concatenate([before, value[: BLOCK - 8]], axis=0).astype(BF16)
+        odd[s, pl.ds(pl.multiple_of((i + 1) * BLOCK, 16), 16), :] = jnp.concatenate(
+            [late, jnp.zeros_like(late)], axis=0
+        ).astype(BF16)
+        tail_rows[...] = late
+
+    def taps(even, odd, s, first, count, sign):
+        out = []
+        for k in range(KERNEL_TAPS):
+            off = sign * DILATION_STRIDE * (k - KERNEL_TAPS // 2)
+            buf, base = (even, HALO) if off % 16 == 0 else (odd, 8)
+            at = base + off + first
+            at = at if isinstance(at, int) else pl.multiple_of(at, 16)
+            out.append(buf[s, pl.ds(at, count), :])
+        return out
+
+    def second(s, i):
+        at = pl.ds(pl.multiple_of(s * seq + i * BLOCK, BLOCK), BLOCK)
+        n, rs = stats(dot_nt(act_a[at, :], flat(w_in)))
+        n_b[at, :] = n.astype(BF16)
+        scale[at, 1:2] = rs
+        a = jnp.where(kept(s, i * BLOCK, BLOCK), gelu(n * gain_b + bias_b), 0.0)
+        shifted_store(b_even, b_odd, s, i, a)
+
+    for s in range(slots):
+        hooks = {blocks - 1: [gather["conv"].from_x, gather["conv"].from_y]} if s == 0 else None
+        loop(blocks, functools.partial(second, s), hooks)
+    gather["conv"].from_diagonal()
+    gather["out"].own()
+    gather["conv"].from_sibling()
+
+    def phase_three(n_c, token_rows):
+        def third(s, i):
+            at = pl.ds(pl.multiple_of(s * seq + i * BLOCK, BLOCK), BLOCK)
+            stacked = jnp.concatenate(taps(b_even, b_odd, s, i * BLOCK, BLOCK, 1), axis=1)
+            n, rs = stats(dot_nt(stacked, flat(w_conv)))
+            n_c[at, :] = n.astype(BF16)
+            scale[at, 2:3] = rs
+            act_c[at, :] = jnp.where(kept(s, i * BLOCK, BLOCK), gelu(n * gain_c + bias_c), 0.0).astype(BF16)
+
+        for s in range(slots):
+            hooks = (
+                {1: [gather["out"].from_x, gather["out"].from_y], blocks - 1: [gather["out"].from_diagonal]}
+                if s == slots - 1
+                else None
+            )
+            loop(blocks, functools.partial(third, s), hooks)
+        gather["out"].from_sibling()
+
+        def mixed_copy(j):
+            k = lax.rem(j, 3)
+            return pltpu.make_async_copy(token_rows.at[k], r.mixed.at[block(j, BLOCK), :], r.io.at[2 + k])
+
+        def token_copy(j):
+            k = lax.rem(j, 3)
+            return pltpu.make_async_copy(tokens.at[block(j, BLOCK), :], token_rows.at[k], r.io.at[5 + k])
+
+        token_copy(0).start()
+
+        def fourth(s, i):
+            j = s * blocks + i
+            at = block(j, BLOCK)
+            last = slots * blocks - 1
+
+            @pl.when(j >= 2)
+            def _():
+                mixed_copy(j - 2).wait()
+
+            @pl.when(j < last)
+            def _():
+                token_copy(j + 1).start()
+
+            k = lax.rem(j, 3)
+            hid_c = dot_nt(act_c[at, :], flat(w_out))
+            token_copy(j).wait()
+            token_rows[k] = (token_rows[k].astype(F32) + hid_c).astype(BF16)
+            mixed_copy(j).start()
+            e = jnp.where(kept(s, i * BLOCK, BLOCK), dot_nn(cot[at, :], flat(w_out)), 0.0)
+            back = norm_back(n_c[at, :].astype(F32), scale[at, 2:3], gain_c, bias_c, e, sums, 4)
+            shifted_store(g_even, g_odd, s, i, back)
+            back_t[:, at] = back.astype(BF16).T
+
+        load_cot.wait()
+        for s in range(slots):
+            loop(blocks, functools.partial(fourth, s))
+        mixed_copy(slots * blocks - 2).wait()
+        mixed_copy(slots * blocks - 1).wait()
+
+        chunk = 256
+        tall = r.g_out.shape[3]
+
+        def out_grad(lo):
+            part = dot_tn(cot[:, lo : lo + chunk], act_c[...]).astype(BF16)
+            for f in range(lo // tall, -(-(lo + chunk) // tall)):
+                a, b = max(lo, f * tall), min(lo + chunk, (f + 1) * tall)
+                r.g_out[f // 4, (f // 2) % 2, f % 2, a - f * tall : b - f * tall, :] = part[a - lo : b - lo]
+
+        for lo in range(0, width, chunk):
+            once(out_grad, lo)
+
+    pl.run_scoped(
+        phase_three,
+        pltpu.VMEM((rows, inner), BF16),
+        pltpu.VMEM((3, BLOCK, width), BF16),
+    )
+
+    def scatter_of(n, g):
+        return Scatter(
+            pc, n, g, getattr(r, "rcv_" + n), getattr(r, "r1a_" + n), getattr(r, "r1b_" + n), getattr(r, "r2a_" + n), getattr(r, "r2b_" + n), getattr(r, "zg_" + n),
+            getattr(r, "zr_" + n), getattr(r, "ss_" + n), getattr(r, "sr_" + n),
+        )
+
+    for c in [norm_gather] + [gather[n] for n in NAMES]:
+        c.finish()
+
+    def phase_five(g_in, g_conv):
+        sc_out = scatter_of("out", r.g_out)
+        sc_conv = scatter_of("conv", g_conv)
+        sc_in = scatter_of("in", g_in)
+        sc_out.start()
+        def conv_grad(k):
+            off = DILATION_STRIDE * (k - KERNEL_TAPS // 2)
+            buf, base = (b_even, HALO) if off % 16 == 0 else (b_odd, 8)
+            for lo in range(0, inner, CONV_LANES):
+                hi = min(lo + CONV_LANES, inner)
+                total = None
+                for s in range(slots):
+                    p = dot_nn(back_t[:, s * seq : (s + 1) * seq], buf[s, base + off : base + off + seq, lo:hi])
+                    total = p if total is None else total + p
+                g_conv[:, :, :, :, k * inner + lo : k * inner + hi] = total.astype(BF16).reshape(
+                    (2, 2, 2, inner // PLANE, hi - lo)
+                )
+
+        for k in range(KERNEL_TAPS):
+            once(conv_grad, k)
+            if k == 1:
+                sc_out.step1()
+        sc_conv.start()
+
+        def sixth(s, i):
+            at = block(s * blocks + i, BLOCK)
+            xs = taps(g_even, g_odd, s, i * BLOCK, BLOCK, -1)
+            e = None
+            for k in range(KERNEL_TAPS):
+                wk = w_conv[:, :, :, :, k * inner : (k + 1) * inner].reshape(inner, inner)
+                p = dot_nn(xs[k], wk)
+                e = p if e is None else e + p
+            e = jnp.where(kept(s, i * BLOCK, BLOCK), e, 0.0)
+            back = norm_back(n_b[at, :].astype(F32), scale[at, 1:2], gain_b, bias_b, e, sums, 2).astype(BF16)
+            grad_a[at, :] = back
+            back_t[:, at] = back.T
+
+        for s in range(slots):
+            if s == 0:
+                hooks = {0: [sc_out.step2], 1: [sc_conv.step1], blocks - 1: [sc_out.step3]}
+            else:
+                hooks = {1: [lambda: sc_out.step4(r.s_out)], blocks - 1: [sc_conv.step2]}
+            loop(blocks, functools.partial(sixth, s), hooks)
+
+        chunk = 256
+        n_chunks = width // chunk
+
+        def in_grad(j):
+            part = dot_nn(back_t[...], act_a[:, j * chunk : (j + 1) * chunk]).astype(BF16)
+            g_in[:, :, :, :, j * chunk : (j + 1) * chunk] = part.reshape(2, 2, 2, inner // PLANE, chunk)
+
+        for j in range(n_chunks):
+            once(in_grad, j)
+        sc_in.start()
+
+        def out_copy(at):
+            return pltpu.make_async_copy(cot.at[at, :], r.grad_tokens.at[at, :], r.io.at[8])
+
+        def eighth(i):
+            at = block(i, BLOCK)
+            e = dot_nn(grad_a[at, :], flat(w_in))
+            back = norm_back(x[at, :].astype(F32), scale[at, 0:1], gain_a, bias_a, e, sums, 0)
+            cot[at, :] = (cot[at, :].astype(F32) + back).astype(BF16)
+            out_copy(at).start()
+
+        n_eight = rows // BLOCK
+        hooks = {
+            0: [sc_in.step1],
+            1: [sc_conv.step3],
+            3: [sc_in.step2],
+            5: [lambda: sc_conv.step4(r.s_conv)],
+            6: [sc_in.step3],
+        }
+        loop(n_eight, eighth, hooks)
+        first = small.acc
+        first[0] = jnp.concatenate(
+            [
+                sums[0:1, 0:inner],
+                sums[0:1, inner : 2 * inner],
+                sums[1:2, 0:inner],
+                sums[1:2, inner : 2 * inner],
+                sums[2:6, 0:inner],
+                counts,
+                jnp.zeros((7, inner), F32),
+            ],
+            axis=0,
+        )
+        small.start()
+        sc_in.step4(r.s_in)
+        for k in range(3):
+            small.next(k)
+        total = small.total()
+        r.s_counts[...] = total[8:16, 0:128]
+        mine = jnp.zeros((8, cols), F32)
+        for f in range(PLANE):
+            mine = mine + jnp.where(pc.f == f, total[0:8, f * cols : (f + 1) * cols], 0.0)
+        pair = jnp.zeros((2, cols), F32)
+        for i in range(DP_RANKS):
+            pair = pair + jnp.where(pc.d == i, mine[2 * i : 2 * i + 2], 0.0)
+        r.s_norms[...] = pair
+        for c in (sc_out, sc_conv, sc_in, small):
+            c.finish()
+        pltpu.make_async_copy(cot, r.grad_tokens, r.io.at[8]).wait()
+
+    pl.run_scoped(
+        phase_five,
+        pltpu.VMEM(r.w_in.shape, BF16),
+        pltpu.VMEM(r.w_conv.shape, BF16),
+    )
+
+
+def run_block(tokens, cotangent, lengths, labels, w_in, w_conv, w_out, norm_params):
+    rows, width = tokens.shape
+    cols, rank_in = w_in.shape
+    depth = w_conv.shape[1]
+    inner = cols * PLANE
+    slots = lengths.shape[0]
+    seq = rows // slots
+    V = pltpu.VMEM
+    dma = pltpu.SemaphoreType.DMA
+    shapes = {
+        "in": (cols, width, cols, round_up(rank_in)),
+        "conv": (cols, KERNEL_TAPS * inner, cols, round_up(KERNEL_TAPS * depth)),
+        "out": (w_out.shape[1], inner, w_out.shape[1] // 2, round_up(2 * depth)),
+    }
+    inputs = dict(
+        lens=(lengths, pltpu.SMEM),
+        tokens=(tokens, pl.ANY),
+        cot_in=(cotangent, pl.ANY),
+        labels=(labels.reshape(rows // 128, 128), V),
+        p_in=(w_in, V),
+        p_conv=(w_conv, V),
+        p_out=(w_out, V),
+        p_norms=(norm_params, V),
+    )
+    outputs = dict(
+        mixed=((rows, width), BF16, pl.ANY),
+        grad_tokens=((rows, width), BF16, pl.ANY),
+        s_counts=((8, 128), F32, V),
+        s_norms=(norm_params.shape, F32, V),
+    )
+    scratch = dict(
+        x=V((rows, width), BF16),
+        cot=V((rows, width), BF16),
+        act_a=V((rows, width), BF16),
+        n_b=V((rows, inner), BF16),
+        act_c=V((rows, inner), BF16),
+        scale=V((rows, 8), F32),
+        sums=V((8, width), F32),
+        tail=V((8, inner), F32),
+        norms=V((8, inner), F32),
+        back_t=V((inner, rows), BF16),
+        io=dma((9,)),
+        nz=V((DP_RANKS, 8, 128), F32),
+        nw=V((2, 2, 2, 8, 128), F32),
+        ns=dma((NormGather.SEMS,)),
+        nr=dma((NormGather.SEMS,)),
+        sm_acc=V((4, 16, inner), F32),
+        sm_got=V((3, 16, inner), F32),
+        sm_z=V((DP_RANKS, 16, inner), F32),
+        sm_s=dma((SmallSum.SEMS,)),
+        sm_r=dma((SmallSum.SEMS,)),
+        g_out=V((2, 2, 2) + shapes["out"][:2], BF16),
+    )
+    halo_rows = V((slots, seq + 2 * HALO, inner), BF16)
+    scratch.update(b_even=halo_rows, b_odd=halo_rows, g_even=halo_rows, g_odd=halo_rows)
+    for n, (h, lanes, hz, lz) in shapes.items():
+        outputs["s_" + n] = ((hz, lz), F32, V)
+        size = [
+            tuple(len(range(*c.indices(e))) for c, e in zip(cut, (h, lanes))) for cut in halves(n, (h, lanes))
+        ]
+        scratch["w_" + n] = V((2, 2, 2, h, lanes), BF16)
+        scratch["zg_" + n] = V((DP_RANKS, hz, lz), BF16)
+        scratch["gs_" + n] = dma((Gather.SEMS,))
+        scratch["gr_" + n] = dma((Gather.SEMS,))
+        scratch["rcv_" + n] = V((2, 2, h, lanes), BF16)
+        scratch["r1a_" + n] = V((2,) + size[0], BF16)
+        scratch["r1b_" + n] = V((2,) + size[1], BF16)
+        scratch["r2a_" + n] = V(size[0], BF16)
+        scratch["r2b_" + n] = V(size[1], BF16)
+        scratch["zr_" + n] = V((DP_RANKS, hz, lz), BF16)
+        scratch["ss_" + n] = dma((Scatter.SEMS,))
+        scratch["sr_" + n] = dma((Scatter.SEMS,))
+    names = list(inputs) + list(outputs) + list(scratch)
+    work = 6 * rows * (2 * width * inner + KERNEL_TAPS * inner * inner)
+    out = pl.pallas_call(
+        lambda *refs: block_kernel(SimpleNamespace(**dict(zip(names, refs)))),
+        out_shape=tuple(jax.ShapeDtypeStruct(s, t) for s, t, _ in outputs.values()),
+        in_specs=[pl.BlockSpec(memory_space=m) for _, m in inputs.values()],
+        out_specs=tuple(pl.BlockSpec(memory_space=m) for _, _, m in outputs.values()),
+        scratch_shapes=list(scratch.values()),
+        compiler_params=pltpu.CompilerParams(
+            collective_id=0, has_side_effects=True, vmem_limit_bytes=VMEM_BYTES
+        ),
+        cost_estimate=pl.CostEstimate(flops=work, bytes_accessed=8 * rows * width, transcendentals=0),
+        name="residual_block",
+    )(*(a for a, _ in inputs.values()))
+    return dict(zip(outputs, out))
+
+
+VMEM_BYTES = 63 * 1024 * 1024
+
+
+def finish_kernel(n_copies, refs):
+    r = refs
+    rows = r.mixed.shape[0] // n_copies
+    come, go = [], []
+    for i in range(n_copies):
+        for src, mid, dst in ((r.mixed, r.hold_mixed, r.new_mixed), (r.grad_tokens, r.hold_grad, r.new_grad_tokens)):
+            at = pl.ds(i * rows, rows)
+            sem = r.big_sem.at[len(come)]
+            come.append(pltpu.make_async_copy(src.at[at, :], mid.at[at, :], sem))
+            go.append(pltpu.make_async_copy(mid.at[at, :], dst.at[at, :], sem))
+    loads = {}
+    for n in STEP_ORDER:
+        for kind in ("s_", "w_", "m_", "v_"):
+            k = kind + n
+            loads[k] = pltpu.make_async_copy(getattr(r, k), getattr(r, "b" + k), r.in_sem.at[len(loads)])
+            loads[k].start()
+    loads["s_counts"] = pltpu.make_async_copy(r.s_counts, r.bs_counts, r.in_sem.at[len(loads)])
+    loads["s_counts"].start()
+    for c in come:
+        c.start()
+    stores = []
+
+    def pass_on(first, last):
+        for c, g in zip(come[first:last], go[first:last]):
+            c.wait()
+            g.start()
+
+    def store(k):
+        stores.append(pltpu.make_async_copy(getattr(r, "o" + k), getattr(r, "n" + k), r.out_sem.at[len(stores)]))
+        stores[-1].start()
+
+    def step(n, at, grad, rate, decay):
+        new = adamw(getattr(r, "bw_" + n)[at], getattr(r, "bm_" + n)[at], getattr(r, "bv_" + n)[at], grad, rate, decay)
+        for kind, value in zip(("ow_", "om_", "ov_"), new):
+            getattr(r, kind + n)[at] = value
+
+    def ready(n):
+        for kind in ("s_", "w_", "m_", "v_"):
+            loads[kind + n].wait()
+
+    def done(n):
+        for kind in ("w_", "m_", "v_"):
+            store(kind + n)
+
+    everything = (slice(None), slice(None))
+    ready("conv")
+    depth = r.bw_conv.shape[1]
+    for k in range(KERNEL_TAPS):
+        grad = r.bs_conv[:, k * depth : (k + 1) * depth].T
+        step("conv", (k,), grad, 0.5 * (KERNEL_TAPS * INNER) ** (-0.5), 0.01)
+    done("conv")
+    pass_on(0, n_copies)
+    ready("in")
+    step("in", everything, r.bs_in[:, 0 : r.bw_in.shape[1]], 0.5 * D ** (-0.5), 0.01)
+    done("in")
+    ready("out")
+    flat = r.bs_out[...]
+    grad = jnp.concatenate([flat[:, 0:depth].T, flat[:, depth : 2 * depth].T], axis=1)
+    step("out", everything, grad, 0.5 * (INNER // 2) ** (-0.5), 0.01)
+    done("out")
+    ready("norms")
+    step("norms", everything, r.bs_norms[...], 0.3, 0.0)
+    done("norms")
+    pass_on(n_copies, 2 * n_copies)
+    loads["s_counts"].wait()
+    r.type_counts[...] = r.bs_counts[0, 0:TYPES].astype(jnp.int32)
+    for c in stores + go:
+        c.wait()
+
+
+STEP_ORDER = ("conv", "in", "out", "norms")
+BIG_COPIES = 4
+
+
+def run_finish(res, weights, means, squares):
+    V, dma = pltpu.VMEM, pltpu.SemaphoreType.DMA
+    inputs = {k: res[k] for k in ("mixed", "grad_tokens", "s_counts")}
+    for n in STEP_ORDER:
+        inputs["s_" + n] = res["s_" + n]
+        for kind, arrays in (("w_", weights), ("m_", means), ("v_", squares)):
+            inputs[kind + n] = arrays[n]
+    outputs = {"new_" + k: res[k] for k in ("mixed", "grad_tokens")}
+    for kind in ("w_", "m_", "v_"):
+        for n in ("in", "conv", "out", "norms"):
+            outputs["n" + kind + n] = weights[n]
+    scratch = {}
+    for k, a in inputs.items():
+        if k[1] == "_":
+            scratch["b" + k] = V(a.shape, a.dtype)
+    for k, a in outputs.items():
+        if k[2] == "_":
+            scratch["o" + k[1:]] = V(a.shape, a.dtype)
+    whole = V(res["mixed"].shape, BF16)
+    scratch.update(hold_mixed=whole, hold_grad=whole)
+    scratch.update(in_sem=dma((17,)), out_sem=dma((12,)), big_sem=dma((2 * BIG_COPIES,)))
+    shapes = [jax.ShapeDtypeStruct(a.shape, a.dtype) for a in outputs.values()]
+    names = list(inputs) + list(outputs) + ["type_counts"] + list(scratch)
+    hbm = pl.BlockSpec(memory_space=pl.ANY)
+    out = pl.pallas_call(
+        lambda *refs: finish_kernel(BIG_COPIES, SimpleNamespace(**dict(zip(names, refs)))),
+        out_shape=tuple(shapes) + (jax.ShapeDtypeStruct((TYPES,), jnp.int32),),
+        in_specs=[hbm] * len(inputs),
+        out_specs=(hbm,) * len(outputs) + (pl.BlockSpec(memory_space=V),),
+        scratch_shapes=list(scratch.values()),
+        compiler_params=pltpu.CompilerParams(vmem_limit_bytes=VMEM_BYTES),
+        name="finish",
+    )(*inputs.values())
+    return out
+
+
+def fused_body(
+    tokens,
+    cotangent,
+    lengths,
+    labels,
+    w_in,
+    w_conv,
+    w_out,
+    norm_params,
+    mean_w_in,
+    mean_w_conv,
+    mean_w_out,
+    mean_norms,
+    square_w_in,
+    square_w_conv,
+    square_w_out,
+    square_norms,
+):
+    res = run_block(tokens, cotangent, lengths, labels, w_in.T, w_conv, w_out, norm_params)
+    new = run_finish(
+        res,
+        dict(zip(NAMES + ("norms",), (w_in.T, w_conv, w_out, norm_params))),
+        dict(zip(NAMES + ("norms",), (mean_w_in.T, mean_w_conv, mean_w_out, mean_norms))),
+        dict(zip(NAMES + ("norms",), (square_w_in.T, square_w_conv, square_w_out, square_norms))),
+    )
+    mixed, grad_tokens, *steps, counts = new
+    for i in (0, 4, 8):
+        steps[i] = steps[i].T
+    return (mixed, grad_tokens, counts) + tuple(steps)
+
+
 def solution(mesh):
+    fused = mesh.shape["dp"] == DP_RANKS and mesh.shape["fsdp"] == PLANE
     return jax.shard_map(
-        body,
+        fused_body if fused else plain_body,
         mesh=mesh,
         in_specs=(
             P(("dp", "fsdp"), None),

time: 560 us -> 176 us (0.31)
  waiting for transfers between devices: 192 us -> 0 us
  Pallas kernels: 0 us -> 175 us
  blocking collectives: 111 us -> 0 us
  matrix products: 105 us -> 0 us
  other arithmetic: 74.4 us -> 0 us
  local copies, waits for them, and re-layouts: 56 us -> 0 us
  between operations: 16.2 us -> 0.83 us
    pallas_call x0 -> x2, Pallas kernels: none -> 175 us  [the longest x1 166 us: run_block(): pl.pallas_call(lambda *refs: block_kernel(SimpleNamespace(**dict(zip(name...]
    dot_general x9 -> x0, matrix products: 105 us -> none  [the longest x3 43.2 us: contract_cols(): lax.dot_general(left, right, (((1,), (1,)), ((), ())), preferred_element_...]
    unnamed x14 -> x0, waiting for transfers between devices: 73.7 us -> none
    all_gather x3 -> x0, waiting for transfers between devices: 70.3 us -> none  [the longest x1 35.7 us: gather_params(): lax.all_gather(part[2], 'dp', axis=0, tiled=True)]
    all_gather x5 -> x0, blocking collectives: 60.2 us -> none  [the longest x1 17.7 us: gather_params(): lax.all_gather(second, 'fsdp', axis=2, tiled=True)]
    reduce_scatter x3 -> x0, waiting for transfers between devices: 48.1 us -> none  [the longest x1 45.5 us: reduce_grads(): lax.psum_scatter(third, 'fsdp', scatter_dimension=1, tiled=True)]
    psum x1 -> x0, blocking collectives: 39 us -> none  [body(): type_counts = lax.psum(local_counts, ('dp', 'fsdp'))]
    reduce_sum x9 -> x0, other arithmetic: 30.7 us -> none  [the longest x2 15.1 us: normalize(): return center * lax.rsqrt(spread + EPSILON) * gain + bias]
  transfers between devices with their start and end apart: 10 -> 0, of which waited for: 8 -> 0; matrix products, arithmetic and copies ran while one was open for 25% -> 0% of each run, Pallas kernels for 0% -> 0%
where the time goes in v1:
time: 176 us
  Pallas kernels  175 us (99%)
    pallas_call x1, Pallas kernels, run_block(): pl.pallas_call(lambda *refs: block_kernel(SimpleNamespace(**dict(zip(name...  166 us
    pallas_call x1, Pallas kernels, run_finish(): pl.pallas_call(lambda *refs: finish_kernel(BIG_COPIES, SimpleNamespace(**...  9.71 us

profile of v1, /device:TPU:0, one launch (start us, length us, event | category | flops | bytes accessed | tf_op | source)
XLA Modules:
  0.0 176.1 jit_solution(1967262435080660804)
XLA Ops:
  0.6 165.5 %residual_block.1 = (bf16[2048,1280]{1,0:T(8,128)(2,1)}, bf16[2048,1280]{1,0:T(8,128)(2,1)}, f32[8,128]{1,0:T(8,128)}, f32[2,80]{1,0:T(2,128)}, f32[80,384]{1,0:...) custom-call(s32[2]{0:T(128)} %refs_0_.1, bf16[2048,1280]{1,0:T(8,128)(2,1)} %refs_1_.1, bf16[2048,1280]{1,0:T(8,128)(2,1)} %refs_2_.1, ...), custom_call_target="tpu_custom_call" | custom-call | flops 45298483200 | bytes 20971520 | tf_op jit(solution)/shard_map/residual_block/pallas_call | solution.py:1080
  166.2 9.7 %finish.1 = (bf16[2048,1280]{1,0:T(8,128)(2,1)}, bf16[2048,1280]{1,0:T(8,128)(2,1)}, f32[80,320]{1,0:T(8,128)}, f32[5,160,80]{2,1,0:T(8,128)}, f32[160,160]{1,0:...) custom-call(bf16[2048,1280]{1,0:T(8,128)(2,1)} %get-tuple-element.37, ...), custom_call_target="tpu_custom_call" | custom-call | tf_op jit(solution)/shard_map/finish/pallas_call | solution.py:1196

commit v2 on v1

--- a/solution.py
+++ b/solution.py
@@ -241,8 +241,7 @@
 HALO = (KERNEL_TAPS // 2) * DILATION_STRIDE
 GELU_SCALE, GELU_CUBE = 0.7978845608, 0.044715
 BLOCK = 256
-CONV_LANES = 256
-NAMES = ("in", "conv", "out")
+UNROLL = 2
 
 
 def dot_nn(a, b):
@@ -331,21 +330,36 @@
     )
 
 
-def halves(name, shape):
-    h, lanes = shape[-2:]
-    if name == "out":
-        return (slice(0, h // 2), slice(None)), (slice(h // 2, h), slice(None))
-    cut = round_up(lanes // 2)
-    return (slice(None), slice(0, cut)), (slice(None), slice(cut, lanes))
+class Unit:
+    def __init__(self, name, first=0, count=0):
+        self.name, self.first, self.count = name, first, count
+        self.lead = (pl.ds(first, count),) if count else ()
+        self.taps = [(k,) for k in range(count)] or [()]
+
+    def tap(self, k):
+        return (k[0] + self.first,) if k else ()
+
+    def halves(self, h, lanes):
+        if self.name == "out":
+            return (slice(0, h // 2), slice(None)), (slice(h // 2, h), slice(None))
+        cut = lanes // 2 // 128 * 128
+        if self.first == 0:
+            cut = lanes - cut
+        return (slice(None), slice(0, cut)), (slice(None), slice(cut, lanes))
+
+    def sizes(self, h, lanes):
+        return [tuple(len(range(*c.indices(e))) for c, e in zip(cut, (h, lanes))) for cut in self.halves(h, lanes)]
+
+
+UNITS = (Unit("in"), Unit("c0", 0, 3), Unit("c1", 3, 2), Unit("out"))
 
 
 class Gather:
     SEMS = 13
 
-    def __init__(self, pc, name, w, zr, send, recv):
-        self.pc, self.w, self.zr, self.send, self.recv = pc, w, zr, send, recv
-        self.name = name
-        self.cut = halves(name, w.shape)
+    def __init__(self, pc, unit, w, zr, send, recv):
+        self.pc, self.unit, self.w, self.zr, self.send, self.recv = pc, unit, w, zr, send, recv
+        self.cut = unit.halves(*w.shape[-2:])
         self.sent = []
 
     def z(self, j):
@@ -371,18 +385,32 @@
         remote(ref, ref, self.send.at[i], self.recv.at[i], self.pc.sib).wait_recv()
 
     def at(self, y, x, c, half=None):
-        r = self.w.at[y, x, c]
-        return r if half is None else r.at[self.cut[half]]
+        part = self.cut[half] if half is not None else (slice(None), slice(None))
+        return self.w.at[self.unit.lead + (y, x, c) + part]
 
     def own(self):
         pc = self.pc
         for j in range(1, DP_RANKS):
             self.z_in(j).wait_recv()
-        ASSEMBLE[self.name](self.w, self.zr, (pc.y, pc.x, pc.c))
+        self.assemble()
         mine = self.at(pc.y, pc.x, pc.c)
         self.go(mine, 4, pc.xn)
         self.go(mine, 5, pc.yn)
         self.go(mine, 8, pc.sib)
+
+    def assemble(self):
+        own = (self.pc.y, self.pc.x, self.pc.c)
+        h = self.zr.shape[1]
+        n = self.w.shape[-1] // DP_RANKS
+        pieces = [self.zr[i] for i in range(DP_RANKS)]
+        if self.unit.name == "out":
+            for part in range(2):
+                joined = jnp.concatenate([p[:, part * n : (part + 1) * n] for p in pieces], axis=1)
+                self.w[own + (slice(part * h, (part + 1) * h),)] = joined
+            return
+        for k in self.unit.taps:
+            at = k[0] * n if k else 0
+            self.w[self.unit.tap(k) + own] = jnp.concatenate([p[:, at : at + n] for p in pieces], axis=1)
 
     def from_x(self):
         pc = self.pc
@@ -421,70 +449,42 @@
             remote(ref, ref, self.send.at[i], self.recv.at[i], device).wait_send()
 
 
-def assemble_in(w, zr, own):
-    n = w.shape[-1] // DP_RANKS
-    w[own] = jnp.concatenate([zr[i][:, :n] for i in range(DP_RANKS)], axis=1)
-
-
-def assemble_conv(w, zr, own):
-    n = w.shape[-1] // (DP_RANKS * KERNEL_TAPS)
-    w[own] = jnp.concatenate(
-        [zr[i][:, k * n : (k + 1) * n] for k in range(KERNEL_TAPS) for i in range(DP_RANKS)], axis=1
-    )
-
-
-def assemble_out(w, zr, own):
-    n = w.shape[-1] // DP_RANKS
-    h = zr.shape[1]
-    for part in range(2):
-        w[own + (slice(part * h, (part + 1) * h),)] = jnp.concatenate(
-            [zr[i][:, part * n : (part + 1) * n] for i in range(DP_RANKS)], axis=1
-        )
-
-
-ASSEMBLE = {"in": assemble_in, "conv": assemble_conv, "out": assemble_out}
-
-
 class Scatter:
     SEMS = 9
 
-    def __init__(self, pc, name, g, rcv, r1a, r1b, r2a, r2b, zs, zr, send, recv):
-        self.pc, self.name, self.g, self.rcv = pc, name, g, rcv
+    def __init__(self, pc, unit, g, rcv, r1a, r1b, r2a, r2b, zs, zr, send, recv):
+        self.pc, self.unit, self.g, self.rcv = pc, unit, g, rcv
         self.r1a, self.r1b, self.r2a, self.r2b = r1a, r1b, r2a, r2b
         self.zs, self.zr, self.send, self.recv = zs, zr, send, recv
-        self.cut = halves(name, g.shape)
-
-    def copy(self, i, src, dst, device):
-        return remote(src, dst, self.send.at[i], self.recv.at[i], device)
-
-    def half(self, ref, k):
-        return ref.at[(slice(None),) * (len(ref.shape) - 2) + self.cut[k]]
+        self.cut = unit.halves(*g.shape[-2:])
+
+    def copy(self, i, at, dst, device):
+        return remote(self.g.at[self.unit.lead + at], dst, self.send.at[i], self.recv.at[i], device)
 
     def c0(self):
         pc = self.pc
-        return self.copy(0, self.g.at[:, :, pc.oc], self.rcv, pc.sib)
+        every = slice(None)
+        return self.copy(0, (every, every, pc.oc), self.rcv, pc.sib)
 
     def a1(self):
         pc = self.pc
-        return self.copy(1, self.half(self.g.at[:, pc.ox, pc.c], 0), self.r1a, pc.xn)
+        return self.copy(1, (slice(None), pc.ox, pc.c) + self.cut[0], self.r1a, pc.xn)
 
     def b1(self):
         pc = self.pc
-        return self.copy(2, self.half(self.g.at[pc.oy, :, pc.c], 1), self.r1b, pc.yn)
+        return self.copy(2, (pc.oy, slice(None), pc.c) + self.cut[1], self.r1b, pc.yn)
 
     def a2(self):
         pc = self.pc
-        return self.copy(3, self.half(self.g.at[pc.oy, pc.x, pc.c], 0), self.r2a, pc.yn)
+        return self.copy(3, (pc.oy, pc.x, pc.c) + self.cut[0], self.r2a, pc.yn)
 
     def b2(self):
         pc = self.pc
-        return self.copy(4, self.half(self.g.at[pc.y, pc.ox, pc.c], 1), self.r2b, pc.xn)
+        return self.copy(4, (pc.y, pc.ox, pc.c) + self.cut[1], self.r2b, pc.xn)
 
     def z(self, j):
         pc = self.pc
-        return remote(
-            self.zs.at[pc.ranks[j]], self.zr.at[pc.d], self.send.at[4 + j], self.recv.at[5 + pc.d], pc.zn[j - 1]
-        )
+        return remote(self.zs.at[pc.ranks[j]], self.zr.at[pc.d], self.send.at[4 + j], self.recv.at[5 + pc.d], pc.zn[j - 1])
 
     def z_in(self, j):
         pc = self.pc
@@ -493,40 +493,57 @@
 
     def start(self):
         self.c0().start()
+
+    def add(self, at, ref, ref_at):
+        for k in self.unit.taps:
+            idx = self.unit.tap(k) + at
+            self.g[idx] = (self.g[idx].astype(F32) + ref[k + ref_at].astype(F32)).astype(BF16)
 
     def step1(self):
         pc = self.pc
         self.c0().wait_recv()
         for y in range(2):
             for x in range(2):
-                self.g[y, x, pc.c] = (self.g[y, x, pc.c].astype(F32) + self.rcv[y, x].astype(F32)).astype(BF16)
+                self.add((y, x, pc.c), self.rcv, (y, x))
         self.a1().start()
         self.b1().start()
 
-    def add(self, y, x, k, ref):
-        idx = (y, x, self.pc.c) + self.cut[k]
-        self.g[idx] = (self.g[idx].astype(F32) + ref[...].astype(F32)).astype(BF16)
-
     def step2(self):
         pc = self.pc
+        own = (pc.y, pc.x, pc.c)
         self.a1().wait_recv()
-        self.add(pc.oy, pc.x, 0, self.r1a.at[pc.oy])
+        self.add((pc.oy, pc.x, pc.c) + self.cut[0], self.r1a, (pc.oy,))
         self.a2().start()
         self.b1().wait_recv()
-        self.add(pc.y, pc.ox, 1, self.r1b.at[pc.ox])
+        self.add((pc.y, pc.ox, pc.c) + self.cut[1], self.r1b, (pc.ox,))
         self.b2().start()
-        self.add(pc.y, pc.x, 0, self.r1a.at[pc.y])
-        self.add(pc.y, pc.x, 1, self.r1b.at[pc.x])
+        self.add(own + self.cut[0], self.r1a, (pc.y,))
+        self.add(own + self.cut[1], self.r1b, (pc.x,))
 
     def step3(self):
         pc = self.pc
+        own = (pc.y, pc.x, pc.c)
         self.a2().wait_recv()
-        self.add(pc.y, pc.x, 0, self.r2a)
+        self.add(own + self.cut[0], self.r2a, ())
         self.b2().wait_recv()
-        self.add(pc.y, pc.x, 1, self.r2b)
-        SPLIT[self.name](self.zs, self.g[pc.y, pc.x, pc.c])
+        self.add(own + self.cut[1], self.r2b, ())
+        self.split(own)
         for j in (2, 1, 3):
             self.z(j).start()
+
+    def split(self, own):
+        h = self.zs.shape[1]
+        n = self.g.shape[-1] // DP_RANKS
+        if self.unit.name == "out":
+            v = self.g[own]
+            for i in range(DP_RANKS):
+                at = slice(i * n, (i + 1) * n)
+                self.zs[i, :, 0 : 2 * n] = jnp.concatenate([v[0:h, at], v[h : 2 * h, at]], axis=1)
+            return
+        parts = [self.g[self.unit.tap(k) + own] for k in self.unit.taps]
+        for i in range(DP_RANKS):
+            at = slice(i * n, (i + 1) * n)
+            self.zs[i, :, 0 : len(parts) * n] = jnp.concatenate([v[:, at] for v in parts], axis=1)
 
     def step4(self, out):
         pc = self.pc
@@ -541,31 +558,6 @@
             c.wait_send()
         for j in range(1, DP_RANKS):
             self.z(j).wait_send()
-
-
-def split_in(zs, v):
-    n = v.shape[1] // DP_RANKS
-    for i in range(DP_RANKS):
-        zs[i, :, 0:n] = v[:, i * n : (i + 1) * n]
-
-
-def split_conv(zs, v):
-    n = v.shape[1] // (DP_RANKS * KERNEL_TAPS)
-    for i in range(DP_RANKS):
-        starts = [(DP_RANKS * k + i) * n for k in range(KERNEL_TAPS)]
-        zs[i, :, 0 : KERNEL_TAPS * n] = jnp.concatenate([v[:, s : s + n] for s in starts], axis=1)
-
-
-def split_out(zs, v):
-    n = v.shape[1] // DP_RANKS
-    h = zs.shape[1]
-    for i in range(DP_RANKS):
-        zs[i, :, 0 : 2 * n] = jnp.concatenate(
-            [v[0:h, i * n : (i + 1) * n], v[h : 2 * h, i * n : (i + 1) * n]], axis=1
-        )
-
-
-SPLIT = {"in": split_in, "conv": split_conv, "out": split_out}
 
 
 class NormGather:
@@ -671,27 +663,34 @@
     return r * (dn - m1 - n * m2)
 
 
-def block_kernel(refs):
-    r = refs
+def block_kernel(r):
     pc = Place()
-    tokens, cot_in, lens, labels = r.tokens, r.cot_in, r.lens, r.labels
     x, cot, act_a, n_b, act_c = r.x, r.cot, r.act_a, r.n_b, r.act_c
     scale, sums, tail_rows = r.scale, r.sums, r.tail
     b_even, b_odd, g_even, g_odd, back_t = r.b_even, r.b_odd, r.g_even, r.g_odd, r.back_t
     rows, width = x.shape
     inner = n_b.shape[1]
-    slots = lens.shape[0]
+    slots = r.lens.shape[0]
     seq = rows // slots
     blocks = seq // BLOCK
     grad_a = act_c
 
-    wide = {"in": r.w_in, "conv": r.w_conv, "out": r.w_out}
-    gather = {n: Gather(pc, n, wide[n], getattr(r, "zg_" + n), getattr(r, "gs_" + n), getattr(r, "gr_" + n)) for n in NAMES}
+    wide = dict(zip([u.name for u in UNITS], (r.w_in, r.w_conv, r.w_conv, r.w_out)))
+    own = {u.name: SimpleNamespace(**{k: getattr(r, k + u.name) for k in UNIT_SCRATCH}) for u in UNITS}
+    pull = [Gather(pc, u, wide[u.name], own[u.name].zg_, own[u.name].gs_, own[u.name].gr_) for u in UNITS]
+    get_in, get_c0, get_c1, get_out = pull
+
+    def scatter(u, g):
+        m = own[u.name]
+        return Scatter(pc, u, g, m.rcv_, m.r1a_, m.r1b_, m.r2a_, m.r2b_, m.zg_, m.zr_, m.ss_, m.sr_)
+
     norm_gather = NormGather(pc, r.nz, r.nw, r.ns, r.nr)
     small = SmallSum(pc, r.sm_acc, r.sm_got, r.sm_z, r.sm_s, r.sm_r)
 
-    load_x = pltpu.make_async_copy(tokens, x, r.io.at[0])
-    load_cot = pltpu.make_async_copy(cot_in, cot, r.io.at[1])
+    load_x = pltpu.make_async_copy(r.tokens, x, r.io.at[0])
+    load_cot = pltpu.make_async_copy(r.cot_in, cot, r.io.at[1])
+    save_act = pltpu.make_async_copy(act_c, r.act_out, r.io.at[2])
+    save_w = pltpu.make_async_copy(r.w_out, r.w_saved, r.io.at[3])
     load_x.start()
 
     cols = r.p_in.shape[0]
@@ -699,10 +698,11 @@
     barrier(pc)
     norm_gather.start()
     r.zg_in[pc.d, :, 0 : r.p_in.shape[1]] = r.p_in[...].astype(BF16)
-    gather["in"].start()
+    get_in.start()
     depth = r.p_conv.shape[1]
-    for k in range(KERNEL_TAPS):
-        r.zg_conv[pc.d, :, k * depth : (k + 1) * depth] = r.p_conv[k].T.astype(BF16)
+    for g in (get_c0, get_c1):
+        for k in range(g.unit.count):
+            g.zr[pc.d, :, k * depth : (k + 1) * depth] = r.p_conv[g.unit.first + k].T.astype(BF16)
     p_out = r.p_out[...].T.astype(BF16)
     h_out = r.zg_out.shape[1]
     r.zg_out[pc.d, :, 0 : 2 * depth] = jnp.concatenate([p_out[0:h_out], p_out[h_out : 2 * h_out]], axis=1)
@@ -715,24 +715,26 @@
             buf[s, seq + HALO : seq + 2 * HALO, :] = pad
 
     def kept(s, first, count):
-        return first + lax.broadcasted_iota(jnp.int32, (count, 1), 0) < lens[s]
-
-    lab = labels[...]
+        return first + lax.broadcasted_iota(jnp.int32, (count, 1), 0) < r.lens[s]
+
+    lab = r.labels[...]
     place = (
         lax.broadcasted_iota(jnp.int32, lab.shape, 0) * lab.shape[1] + lax.broadcasted_iota(jnp.int32, lab.shape, 1)
     )
     valid = place < 0
     for s in range(slots):
-        valid = valid | ((place >= s * seq) & (place < s * seq + lens[s]))
+        valid = valid | ((place >= s * seq) & (place < s * seq + r.lens[s]))
     lane = lax.broadcasted_iota(jnp.int32, (1, inner), 1)
     counts = jnp.zeros((1, inner), F32)
     for c in range(TYPES):
         hits = jnp.sum(jnp.where(valid & (lab == c), 1.0, 0.0), keepdims=True)
         counts = counts + jnp.where(lane == c, hits, 0.0)
+    small.acc[0, 8:9, :] = counts
 
     load_x.wait()
     load_cot.start()
     strip = BLOCK // 2
+    strips = rows // strip
 
     def first_stats(i):
         at = block(i, strip)
@@ -740,12 +742,17 @@
         x[at, :] = n.astype(BF16)
         scale[at, 0:1] = rs
 
-    loop(rows // strip, first_stats)
-    norm_gather.own()
-    gather["in"].own()
-    gather["conv"].start()
-    for k in range(3):
-        norm_gather.next(k)
+    loop(
+        strips,
+        first_stats,
+        {
+            strips // 4: [norm_gather.own],
+            strips // 2: [lambda: norm_gather.next(0)],
+            strips * 3 // 4: [get_c0.start, lambda: norm_gather.next(1)],
+        },
+    )
+    norm_gather.next(2)
+    get_in.own()
     r.norms[...] = norm_gather.whole(cols)
     norms = r.norms
     gain_a = jnp.concatenate([norms[0:1, :], norms[1:2, :]], axis=1)
@@ -756,116 +763,117 @@
         at = block(i, strip)
         act_a[at, :] = gelu(x[at, :].astype(F32) * gain_a + bias_a).astype(BF16)
 
-    half_way = rows // strip // 2
-    loop(half_way, first_act)
-    gather["in"].from_x()
-    gather["in"].from_y()
-    loop(half_way, lambda i: first_act(i + half_way))
-    gather["in"].from_diagonal()
-    gather["conv"].own()
-    gather["out"].start()
-    gather["in"].from_sibling()
-    w_in = r.w_in
-    w_conv = r.w_conv
-    w_out = r.w_out
+    loop(strips, first_act)
+    get_in.from_x()
+    get_in.from_y()
+    get_c0.own()
+    get_c1.start()
+    get_in.from_diagonal()
+    get_in.from_sibling()
+    w_in, w_conv, w_out = r.w_in, r.w_conv, r.w_out
 
     def flat(w):
         v = w[...]
         return v.reshape(PLANE * v.shape[3], v.shape[4])
 
-    def shifted_store(even, odd, s, i, value):
-        even[s, pl.ds(pl.multiple_of(i * BLOCK + HALO, 16), BLOCK), :] = value.astype(BF16)
-        before = jnp.where(i == 0, 0.0, tail_rows[...])
+    def skewed(steps, multiply, rest, hooks=None):
+        def step(j):
+            ahead = multiply(j * UNROLL)
+            for u in range(UNROLL):
+                now = ahead
+                if u + 1 < UNROLL:
+                    ahead = multiply(j * UNROLL + u + 1)
+                rest(j * UNROLL + u, now)
+
+        step.__name__ = multiply.__name__
+        loop(steps // UNROLL, step, hooks)
+
+    def place_of(j):
+        return j // blocks, lax.rem(j, blocks) * BLOCK
+
+    def shifted_store(even, odd, j, value):
+        s, first = place_of(j)
+        even[s, pl.ds(pl.multiple_of(first + HALO, 16), BLOCK), :] = value.astype(BF16)
+        before = jnp.where(first == 0, 0.0, tail_rows[...])
         late = value[BLOCK - 8 :]
-        odd[s, block(i, BLOCK), :] = jnp.concatenate([before, value[: BLOCK - 8]], axis=0).astype(BF16)
-        odd[s, pl.ds(pl.multiple_of((i + 1) * BLOCK, 16), 16), :] = jnp.concatenate(
+        odd[s, pl.ds(pl.multiple_of(first, 16), BLOCK), :] = jnp.concatenate(
+            [before, value[: BLOCK - 8]], axis=0
+        ).astype(BF16)
+        odd[s, pl.ds(pl.multiple_of(first + BLOCK, 16), 16), :] = jnp.concatenate(
             [late, jnp.zeros_like(late)], axis=0
         ).astype(BF16)
         tail_rows[...] = late
 
-    def taps(even, odd, s, first, count, sign):
+    def tap_of(even, odd, k, sign):
+        off = sign * DILATION_STRIDE * (k - KERNEL_TAPS // 2)
+        return (even, HALO + off) if off % 16 == 0 else (odd, 8 + off)
+
+    def taps(even, odd, j, sign):
+        s, first = place_of(j)
         out = []
         for k in range(KERNEL_TAPS):
-            off = sign * DILATION_STRIDE * (k - KERNEL_TAPS // 2)
-            buf, base = (even, HALO) if off % 16 == 0 else (odd, 8)
-            at = base + off + first
-            at = at if isinstance(at, int) else pl.multiple_of(at, 16)
-            out.append(buf[s, pl.ds(at, count), :])
-        return out
-
-    def second(s, i):
-        at = pl.ds(pl.multiple_of(s * seq + i * BLOCK, BLOCK), BLOCK)
-        n, rs = stats(dot_nt(act_a[at, :], flat(w_in)))
+            buf, base = tap_of(even, odd, k, sign)
+            out.append(buf[s, pl.ds(pl.multiple_of(first + base, 16), BLOCK), :])
+        return jnp.concatenate(out, axis=1)
+
+    def kept_in(j):
+        s, first = place_of(j)
+        return kept(s, first, BLOCK)
+
+    total_blocks = slots * blocks
+
+    def second(j):
+        return dot_nt(act_a[block(j, BLOCK), :], flat(w_in))
+
+    def second_rest(j, h):
+        at = block(j, BLOCK)
+        n, rs = stats(h)
         n_b[at, :] = n.astype(BF16)
         scale[at, 1:2] = rs
-        a = jnp.where(kept(s, i * BLOCK, BLOCK), gelu(n * gain_b + bias_b), 0.0)
-        shifted_store(b_even, b_odd, s, i, a)
-
-    for s in range(slots):
-        hooks = {blocks - 1: [gather["conv"].from_x, gather["conv"].from_y]} if s == 0 else None
-        loop(blocks, functools.partial(second, s), hooks)
-    gather["conv"].from_diagonal()
-    gather["out"].own()
-    gather["conv"].from_sibling()
-
-    def phase_three(n_c, token_rows):
-        def third(s, i):
-            at = pl.ds(pl.multiple_of(s * seq + i * BLOCK, BLOCK), BLOCK)
-            stacked = jnp.concatenate(taps(b_even, b_odd, s, i * BLOCK, BLOCK, 1), axis=1)
-            n, rs = stats(dot_nt(stacked, flat(w_conv)))
+        shifted_store(b_even, b_odd, j, jnp.where(kept_in(j), gelu(n * gain_b + bias_b), 0.0))
+
+    loop_end = total_blocks // UNROLL - 1
+    chunk = 256
+    skewed(
+        total_blocks,
+        second,
+        second_rest,
+        {0: [get_c0.from_x, get_c0.from_y], 1: [get_c1.own, get_out.start], loop_end: [get_c0.from_diagonal]},
+    )
+    get_c1.from_x()
+    get_c1.from_y()
+    get_out.own()
+    get_c1.from_diagonal()
+    get_c0.from_sibling()
+    get_c1.from_sibling()
+
+    def conv_rows():
+        v = [w_conv[k].reshape(inner, inner) for k in range(KERNEL_TAPS)]
+        return v
+
+    def third(j):
+        return dot_nt(taps(b_even, b_odd, j, 1), jnp.concatenate(conv_rows(), axis=1))
+
+    def middle(n_c):
+        def third_rest(j, h):
+            at = block(j, BLOCK)
+            n, rs = stats(h)
             n_c[at, :] = n.astype(BF16)
             scale[at, 2:3] = rs
-            act_c[at, :] = jnp.where(kept(s, i * BLOCK, BLOCK), gelu(n * gain_c + bias_c), 0.0).astype(BF16)
-
-        for s in range(slots):
-            hooks = (
-                {1: [gather["out"].from_x, gather["out"].from_y], blocks - 1: [gather["out"].from_diagonal]}
-                if s == slots - 1
-                else None
-            )
-            loop(blocks, functools.partial(third, s), hooks)
-        gather["out"].from_sibling()
-
-        def mixed_copy(j):
-            k = lax.rem(j, 3)
-            return pltpu.make_async_copy(token_rows.at[k], r.mixed.at[block(j, BLOCK), :], r.io.at[2 + k])
-
-        def token_copy(j):
-            k = lax.rem(j, 3)
-            return pltpu.make_async_copy(tokens.at[block(j, BLOCK), :], token_rows.at[k], r.io.at[5 + k])
-
-        token_copy(0).start()
-
-        def fourth(s, i):
-            j = s * blocks + i
-            at = block(j, BLOCK)
-            last = slots * blocks - 1
-
-            @pl.when(j >= 2)
-            def _():
-                mixed_copy(j - 2).wait()
-
-            @pl.when(j < last)
-            def _():
-                token_copy(j + 1).start()
-
-            k = lax.rem(j, 3)
-            hid_c = dot_nt(act_c[at, :], flat(w_out))
-            token_copy(j).wait()
-            token_rows[k] = (token_rows[k].astype(F32) + hid_c).astype(BF16)
-            mixed_copy(j).start()
-            e = jnp.where(kept(s, i * BLOCK, BLOCK), dot_nn(cot[at, :], flat(w_out)), 0.0)
-            back = norm_back(n_c[at, :].astype(F32), scale[at, 2:3], gain_c, bias_c, e, sums, 4)
-            shifted_store(g_even, g_odd, s, i, back)
-            back_t[:, at] = back.astype(BF16).T
-
+            act_c[at, :] = jnp.where(kept_in(j), gelu(n * gain_c + bias_c), 0.0).astype(BF16)
+
+        skewed(
+            total_blocks,
+            third,
+            third_rest,
+            {0: [get_out.from_x, get_out.from_y], 1: [get_out.from_diagonal], loop_end: [get_out.from_sibling]},
+        )
+        save_act.start()
+        save_w.start()
         load_cot.wait()
-        for s in range(slots):
-            loop(blocks, functools.partial(fourth, s))
-        mixed_copy(slots * blocks - 2).wait()
-        mixed_copy(slots * blocks - 1).wait()
-
-        chunk = 256
+        for c in [norm_gather] + pull:
+            c.finish()
+
         tall = r.g_out.shape[3]
 
         def out_grad(lo):
@@ -876,79 +884,81 @@
 
         for lo in range(0, width, chunk):
             once(out_grad, lo)
-
-    pl.run_scoped(
-        phase_three,
-        pltpu.VMEM((rows, inner), BF16),
-        pltpu.VMEM((3, BLOCK, width), BF16),
-    )
-
-    def scatter_of(n, g):
-        return Scatter(
-            pc, n, g, getattr(r, "rcv_" + n), getattr(r, "r1a_" + n), getattr(r, "r1b_" + n), getattr(r, "r2a_" + n), getattr(r, "r2b_" + n), getattr(r, "zg_" + n),
-            getattr(r, "zr_" + n), getattr(r, "ss_" + n), getattr(r, "sr_" + n),
-        )
-
-    for c in [norm_gather] + [gather[n] for n in NAMES]:
-        c.finish()
-
-    def phase_five(g_in, g_conv):
-        sc_out = scatter_of("out", r.g_out)
-        sc_conv = scatter_of("conv", g_conv)
-        sc_in = scatter_of("in", g_in)
-        sc_out.start()
+        put_out = scatter(UNITS[3], r.g_out)
+        put_out.start()
+
+        def fourth(j):
+            return dot_nn(cot[block(j, BLOCK), :], flat(w_out))
+
+        def fourth_rest(j, h):
+            at = block(j, BLOCK)
+            e = jnp.where(kept_in(j), h, 0.0)
+            back = norm_back(n_c[at, :].astype(F32), scale[at, 2:3], gain_c, bias_c, e, sums, 4)
+            shifted_store(g_even, g_odd, j, back)
+            back_t[:, at] = back.astype(BF16).T
+
+        skewed(total_blocks, fourth, fourth_rest, {0: [put_out.step1], 2: [put_out.step2]})
+
+    pl.run_scoped(middle, pltpu.VMEM((rows, inner), BF16))
+    put_out = scatter(UNITS[3], r.g_out)
+
+    def late(g_in, g_conv):
+        put_in, put_c0, put_c1 = scatter(UNITS[0], g_in), scatter(UNITS[1], g_conv), scatter(UNITS[2], g_conv)
+
         def conv_grad(k):
-            off = DILATION_STRIDE * (k - KERNEL_TAPS // 2)
-            buf, base = (b_even, HALO) if off % 16 == 0 else (b_odd, 8)
-            for lo in range(0, inner, CONV_LANES):
-                hi = min(lo + CONV_LANES, inner)
+            buf, base = tap_of(b_even, b_odd, k, 1)
+            for lo in range(0, inner, chunk):
+                hi = min(lo + chunk, inner)
                 total = None
                 for s in range(slots):
-                    p = dot_nn(back_t[:, s * seq : (s + 1) * seq], buf[s, base + off : base + off + seq, lo:hi])
+                    p = dot_nn(back_t[:, s * seq : (s + 1) * seq], buf[s, base : base + seq, lo:hi])
                     total = p if total is None else total + p
-                g_conv[:, :, :, :, k * inner + lo : k * inner + hi] = total.astype(BF16).reshape(
-                    (2, 2, 2, inner // PLANE, hi - lo)
-                )
+                g_conv[k, :, :, :, :, lo:hi] = total.astype(BF16).reshape((2, 2, 2, inner // PLANE, hi - lo))
 
         for k in range(KERNEL_TAPS):
             once(conv_grad, k)
-            if k == 1:
-                sc_out.step1()
-        sc_conv.start()
-
-        def sixth(s, i):
-            at = block(s * blocks + i, BLOCK)
-            xs = taps(g_even, g_odd, s, i * BLOCK, BLOCK, -1)
-            e = None
-            for k in range(KERNEL_TAPS):
-                wk = w_conv[:, :, :, :, k * inner : (k + 1) * inner].reshape(inner, inner)
-                p = dot_nn(xs[k], wk)
-                e = p if e is None else e + p
-            e = jnp.where(kept(s, i * BLOCK, BLOCK), e, 0.0)
+            if k == 0:
+                put_out.step3()
+            if k == 2:
+                put_c0.start()
+            if k == 3:
+                put_c0.step1()
+        put_c1.start()
+        save_act.wait()
+        save_w.wait()
+
+        def sixth(j):
+            return dot_nn(taps(g_even, g_odd, j, -1), w_conv[...].reshape(KERNEL_TAPS * inner, inner))
+
+        def sixth_rest(j, h):
+            at = block(j, BLOCK)
+            e = jnp.where(kept_in(j), h, 0.0)
             back = norm_back(n_b[at, :].astype(F32), scale[at, 1:2], gain_b, bias_b, e, sums, 2).astype(BF16)
             grad_a[at, :] = back
             back_t[:, at] = back.T
 
-        for s in range(slots):
-            if s == 0:
-                hooks = {0: [sc_out.step2], 1: [sc_conv.step1], blocks - 1: [sc_out.step3]}
-            else:
-                hooks = {1: [lambda: sc_out.step4(r.s_out)], blocks - 1: [sc_conv.step2]}
-            loop(blocks, functools.partial(sixth, s), hooks)
-
-        chunk = 256
-        n_chunks = width // chunk
+        skewed(
+            total_blocks,
+            sixth,
+            sixth_rest,
+            {
+                0: [put_c1.step1, lambda: put_out.step4(r.s_out)],
+                1: [put_c0.step2],
+                2: [put_c1.step2],
+                loop_end: [put_c0.step3],
+            },
+        )
 
         def in_grad(j):
             part = dot_nn(back_t[...], act_a[:, j * chunk : (j + 1) * chunk]).astype(BF16)
             g_in[:, :, :, :, j * chunk : (j + 1) * chunk] = part.reshape(2, 2, 2, inner // PLANE, chunk)
 
-        for j in range(n_chunks):
+        for j in range(width // chunk):
             once(in_grad, j)
-        sc_in.start()
+        put_in.start()
 
         def out_copy(at):
-            return pltpu.make_async_copy(cot.at[at, :], r.grad_tokens.at[at, :], r.io.at[8])
+            return pltpu.make_async_copy(cot.at[at, :], r.grad_tokens.at[at, :], r.io.at[4])
 
         def eighth(i):
             at = block(i, BLOCK)
@@ -957,30 +967,28 @@
             cot[at, :] = (cot[at, :].astype(F32) + back).astype(BF16)
             out_copy(at).start()
 
-        n_eight = rows // BLOCK
-        hooks = {
-            0: [sc_in.step1],
-            1: [sc_conv.step3],
-            3: [sc_in.step2],
-            5: [lambda: sc_conv.step4(r.s_conv)],
-            6: [sc_in.step3],
-        }
-        loop(n_eight, eighth, hooks)
-        first = small.acc
-        first[0] = jnp.concatenate(
+        loop(
+            total_blocks,
+            eighth,
+            {
+                0: [put_in.step1, put_c1.step3],
+                2: [lambda: put_c0.step4(r.s_c0)],
+                3: [put_in.step2],
+                4: [lambda: put_c1.step4(r.s_c1)],
+                6: [put_in.step3],
+            },
+        )
+        small.acc[0, 0:8] = jnp.concatenate(
             [
                 sums[0:1, 0:inner],
                 sums[0:1, inner : 2 * inner],
                 sums[1:2, 0:inner],
                 sums[1:2, inner : 2 * inner],
                 sums[2:6, 0:inner],
-                counts,
-                jnp.zeros((7, inner), F32),
             ],
             axis=0,
         )
         small.start()
-        sc_in.step4(r.s_in)
         for k in range(3):
             small.next(k)
         total = small.total()
@@ -992,15 +1000,19 @@
         for i in range(DP_RANKS):
             pair = pair + jnp.where(pc.d == i, mine[2 * i : 2 * i + 2], 0.0)
         r.s_norms[...] = pair
-        for c in (sc_out, sc_conv, sc_in, small):
+        put_in.step4(r.s_in)
+        for c in (put_in, put_c0, put_c1, put_out, small):
             c.finish()
-        pltpu.make_async_copy(cot, r.grad_tokens, r.io.at[8]).wait()
-
-    pl.run_scoped(
-        phase_five,
-        pltpu.VMEM(r.w_in.shape, BF16),
-        pltpu.VMEM(r.w_conv.shape, BF16),
-    )
+
+        def eighth_end(_):
+            pltpu.make_async_copy(cot, r.grad_tokens, r.io.at[4]).wait()
+
+        once(eighth_end, 0)
+
+    pl.run_scoped(late, pltpu.VMEM(r.w_in.shape, BF16), pltpu.VMEM(w_conv.shape, BF16))
+
+
+UNIT_SCRATCH = ("zg_", "gs_", "gr_", "rcv_", "r1a_", "r1b_", "r2a_", "r2b_", "zr_", "ss_", "sr_")
 
 
 def run_block(tokens, cotangent, lengths, labels, w_in, w_conv, w_out, norm_params):
@@ -1012,11 +1024,7 @@
     seq = rows // slots
     V = pltpu.VMEM
     dma = pltpu.SemaphoreType.DMA
-    shapes = {
-        "in": (cols, width, cols, round_up(rank_in)),
-        "conv": (cols, KERNEL_TAPS * inner, cols, round_up(KERNEL_TAPS * depth)),
-        "out": (w_out.shape[1], inner, w_out.shape[1] // 2, round_up(2 * depth)),
-    }
+    h_out = w_out.shape[1]
     inputs = dict(
         lens=(lengths, pltpu.SMEM),
         tokens=(tokens, pl.ANY),
@@ -1028,11 +1036,14 @@
         p_norms=(norm_params, V),
     )
     outputs = dict(
-        mixed=((rows, width), BF16, pl.ANY),
+        act_out=((rows, inner), BF16, pl.ANY),
+        w_saved=((2, 2, 2, h_out, inner), BF16, pl.ANY),
         grad_tokens=((rows, width), BF16, pl.ANY),
         s_counts=((8, 128), F32, V),
         s_norms=(norm_params.shape, F32, V),
     )
+    halo_rows = V((slots, seq + 2 * HALO, inner), BF16)
+    taps = V((KERNEL_TAPS, 2, 2, 2, cols, inner), BF16)
     scratch = dict(
         x=V((rows, width), BF16),
         cot=V((rows, width), BF16),
@@ -1044,7 +1055,15 @@
         tail=V((8, inner), F32),
         norms=V((8, inner), F32),
         back_t=V((inner, rows), BF16),
-        io=dma((9,)),
+        b_even=halo_rows,
+        b_odd=halo_rows,
+        g_even=halo_rows,
+        g_odd=halo_rows,
+        w_in=V((2, 2, 2, cols, width), BF16),
+        w_conv=taps,
+        w_out=V((2, 2, 2, h_out, inner), BF16),
+        g_out=V((2, 2, 2, h_out, inner), BF16),
+        io=dma((5,)),
         nz=V((DP_RANKS, 8, 128), F32),
         nw=V((2, 2, 2, 8, 128), F32),
         ns=dma((NormGather.SEMS,)),
@@ -1054,27 +1073,28 @@
         sm_z=V((DP_RANKS, 16, inner), F32),
         sm_s=dma((SmallSum.SEMS,)),
         sm_r=dma((SmallSum.SEMS,)),
-        g_out=V((2, 2, 2) + shapes["out"][:2], BF16),
-    )
-    halo_rows = V((slots, seq + 2 * HALO, inner), BF16)
-    scratch.update(b_even=halo_rows, b_odd=halo_rows, g_even=halo_rows, g_odd=halo_rows)
-    for n, (h, lanes, hz, lz) in shapes.items():
-        outputs["s_" + n] = ((hz, lz), F32, V)
-        size = [
-            tuple(len(range(*c.indices(e))) for c, e in zip(cut, (h, lanes))) for cut in halves(n, (h, lanes))
-        ]
-        scratch["w_" + n] = V((2, 2, 2, h, lanes), BF16)
-        scratch["zg_" + n] = V((DP_RANKS, hz, lz), BF16)
-        scratch["gs_" + n] = dma((Gather.SEMS,))
-        scratch["gr_" + n] = dma((Gather.SEMS,))
-        scratch["rcv_" + n] = V((2, 2, h, lanes), BF16)
-        scratch["r1a_" + n] = V((2,) + size[0], BF16)
-        scratch["r1b_" + n] = V((2,) + size[1], BF16)
-        scratch["r2a_" + n] = V(size[0], BF16)
-        scratch["r2b_" + n] = V(size[1], BF16)
-        scratch["zr_" + n] = V((DP_RANKS, hz, lz), BF16)
-        scratch["ss_" + n] = dma((Scatter.SEMS,))
-        scratch["sr_" + n] = dma((Scatter.SEMS,))
+    )
+    for u in UNITS:
+        lead = (u.count,) if u.count else ()
+        h, lanes = (cols, width) if u.name == "in" else (h_out, inner) if u.name == "out" else (cols, inner)
+        piece = rank_in if u.name == "in" else depth * (u.count or 2)
+        z = (cols, round_up(piece))
+        half = u.sizes(h, lanes)
+        outputs["s_" + u.name] = (z, F32, V)
+        shapes = (
+            V((DP_RANKS,) + z, BF16),
+            dma((Gather.SEMS,)),
+            dma((Gather.SEMS,)),
+            V(lead + (2, 2, h, lanes), BF16),
+            V(lead + (2,) + half[0], BF16),
+            V(lead + (2,) + half[1], BF16),
+            V(lead + half[0], BF16),
+            V(lead + half[1], BF16),
+            V((DP_RANKS,) + z, BF16),
+            dma((Scatter.SEMS,)),
+            dma((Scatter.SEMS,)),
+        )
+        scratch.update(zip([k + u.name for k in UNIT_SCRATCH], shapes))
     names = list(inputs) + list(outputs) + list(scratch)
     work = 6 * rows * (2 * width * inner + KERNEL_TAPS * inner * inner)
     out = pl.pallas_call(
@@ -1095,35 +1115,31 @@
 VMEM_BYTES = 63 * 1024 * 1024
 
 
-def finish_kernel(n_copies, refs):
-    r = refs
-    rows = r.mixed.shape[0] // n_copies
-    come, go = [], []
-    for i in range(n_copies):
-        for src, mid, dst in ((r.mixed, r.hold_mixed, r.new_mixed), (r.grad_tokens, r.hold_grad, r.new_grad_tokens)):
-            at = pl.ds(i * rows, rows)
-            sem = r.big_sem.at[len(come)]
-            come.append(pltpu.make_async_copy(src.at[at, :], mid.at[at, :], sem))
-            go.append(pltpu.make_async_copy(mid.at[at, :], dst.at[at, :], sem))
+def finish_kernel(r):
+    rows = r.tokens.shape[0] // FINISH_PARTS
     loads = {}
-    for n in STEP_ORDER:
-        for kind in ("s_", "w_", "m_", "v_"):
-            k = kind + n
-            loads[k] = pltpu.make_async_copy(getattr(r, k), getattr(r, "b" + k), r.in_sem.at[len(loads)])
-            loads[k].start()
-    loads["s_counts"] = pltpu.make_async_copy(r.s_counts, r.bs_counts, r.in_sem.at[len(loads)])
-    loads["s_counts"].start()
-    for c in come:
-        c.start()
+
+    def load(k, src, dst):
+        loads[k] = pltpu.make_async_copy(src, dst, r.in_sem.at[len(loads)])
+        loads[k].start()
+
+    load("w", r.w_saved, r.hold_w)
+    parts = [pl.ds(i * rows, rows) for i in range(FINISH_PARTS)]
+    for i, at in enumerate(parts):
+        load(("a", i), r.act_out.at[at, :], r.hold_act.at[at, :])
+        load(("t", i), r.tokens.at[at, :], r.hold_x.at[at, :])
+        load(("g", i), r.grad_tokens.at[at, :], r.hold_g.at[at, :])
+        if i == 0:
+            for n in STEP_ORDER:
+                load("s_" + n, getattr(r, "s_" + n), getattr(r, "bs_" + n))
+                for kind in ("w_", "m_", "v_"):
+                    if n != "c1":
+                        load(kind + n, getattr(r, kind + n), getattr(r, "b" + kind + n))
+            load("n", r.s_counts, r.bs_counts)
     stores = []
 
-    def pass_on(first, last):
-        for c, g in zip(come[first:last], go[first:last]):
-            c.wait()
-            g.start()
-
-    def store(k):
-        stores.append(pltpu.make_async_copy(getattr(r, "o" + k), getattr(r, "n" + k), r.out_sem.at[len(stores)]))
+    def store(src, dst):
+        stores.append(pltpu.make_async_copy(src, dst, r.out_sem.at[len(stores)]))
         stores[-1].start()
 
     def step(n, at, grad, rate, decay):
@@ -1133,68 +1149,92 @@
 
     def ready(n):
         for kind in ("s_", "w_", "m_", "v_"):
-            loads[kind + n].wait()
+            if kind + n in loads:
+                loads[kind + n].wait()
 
     def done(n):
         for kind in ("w_", "m_", "v_"):
-            store(kind + n)
+            store(getattr(r, "o" + kind + n), getattr(r, "n" + kind + n))
 
     everything = (slice(None), slice(None))
-    ready("conv")
-    depth = r.bw_conv.shape[1]
-    for k in range(KERNEL_TAPS):
-        grad = r.bs_conv[:, k * depth : (k + 1) * depth].T
-        step("conv", (k,), grad, 0.5 * (KERNEL_TAPS * INNER) ** (-0.5), 0.01)
-    done("conv")
-    pass_on(0, n_copies)
-    ready("in")
-    step("in", everything, r.bs_in[:, 0 : r.bw_in.shape[1]], 0.5 * D ** (-0.5), 0.01)
-    done("in")
-    ready("out")
-    flat = r.bs_out[...]
-    grad = jnp.concatenate([flat[:, 0:depth].T, flat[:, depth : 2 * depth].T], axis=1)
-    step("out", everything, grad, 0.5 * (INNER // 2) ** (-0.5), 0.01)
-    done("out")
-    ready("norms")
-    step("norms", everything, r.bs_norms[...], 0.3, 0.0)
-    done("norms")
-    pass_on(n_copies, 2 * n_copies)
-    loads["s_counts"].wait()
-    r.type_counts[...] = r.bs_counts[0, 0:TYPES].astype(jnp.int32)
-    for c in stores + go:
+    depth = r.bw_c0.shape[1]
+
+    def conv_step():
+        ready("c0")
+        ready("c1")
+        for u in UNITS[1:3]:
+            for k in range(u.count):
+                grad = getattr(r, "bs_" + u.name)[:, k * depth : (k + 1) * depth].T
+                step("c0", (u.first + k,), grad, 0.5 * (KERNEL_TAPS * INNER) ** (-0.5), 0.01)
+        done("c0")
+
+    def in_step():
+        ready("in")
+        step("in", everything, r.bs_in[:, 0 : r.bw_in.shape[1]], 0.5 * D ** (-0.5), 0.01)
+        done("in")
+
+    def out_step():
+        ready("out")
+        flat = r.bs_out[...]
+        grad = jnp.concatenate([flat[:, 0:depth].T, flat[:, depth : 2 * depth].T], axis=1)
+        step("out", everything, grad, 0.5 * (INNER // 2) ** (-0.5), 0.01)
+        done("out")
+        ready("norms")
+        step("norms", everything, r.bs_norms[...], 0.3, 0.0)
+        done("norms")
+        loads["n"].wait()
+        r.type_counts[...] = r.bs_counts[0, 0:TYPES].astype(jnp.int32)
+
+    others = [conv_step, in_step, out_step]
+    loads["w"].wait()
+    for i, at in enumerate(parts):
+        loads[("a", i)].wait()
+        loads[("t", i)].wait()
+        w = r.hold_w[...]
+        hid = dot_nt(r.hold_act[at, :], w.reshape(PLANE * w.shape[3], w.shape[4]))
+        r.hold_x[at, :] = (r.hold_x[at, :].astype(F32) + hid).astype(BF16)
+        store(r.hold_x.at[at, :], r.new_mixed.at[at, :])
+        loads[("g", i)].wait()
+        store(r.hold_g.at[at, :], r.new_grad_tokens.at[at, :])
+        if i < len(others):
+            others[i]()
+    for c in stores:
         c.wait()
 
 
-STEP_ORDER = ("conv", "in", "out", "norms")
-BIG_COPIES = 4
-
-
-def run_finish(res, weights, means, squares):
+STEP_ORDER = ("c0", "c1", "in", "out", "norms")
+FINISH_PARTS = 4
+
+
+def run_finish(res, tokens, weights, means, squares):
     V, dma = pltpu.VMEM, pltpu.SemaphoreType.DMA
-    inputs = {k: res[k] for k in ("mixed", "grad_tokens", "s_counts")}
+    inputs = {k: res[k] for k in ("act_out", "w_saved", "grad_tokens", "s_counts")}
+    inputs["tokens"] = tokens
+    held = []
     for n in STEP_ORDER:
         inputs["s_" + n] = res["s_" + n]
-        for kind, arrays in (("w_", weights), ("m_", means), ("v_", squares)):
-            inputs[kind + n] = arrays[n]
-    outputs = {"new_" + k: res[k] for k in ("mixed", "grad_tokens")}
+        held.append("s_" + n)
+        if n in weights:
+            for kind, arrays in (("w_", weights), ("m_", means), ("v_", squares)):
+                inputs[kind + n] = arrays[n]
+                held.append(kind + n)
+    outputs = dict(new_mixed=tokens, new_grad_tokens=tokens)
     for kind in ("w_", "m_", "v_"):
-        for n in ("in", "conv", "out", "norms"):
-            outputs["n" + kind + n] = weights[n]
-    scratch = {}
-    for k, a in inputs.items():
-        if k[1] == "_":
-            scratch["b" + k] = V(a.shape, a.dtype)
-    for k, a in outputs.items():
-        if k[2] == "_":
-            scratch["o" + k[1:]] = V(a.shape, a.dtype)
-    whole = V(res["mixed"].shape, BF16)
-    scratch.update(hold_mixed=whole, hold_grad=whole)
-    scratch.update(in_sem=dma((17,)), out_sem=dma((12,)), big_sem=dma((2 * BIG_COPIES,)))
+        for n, a in weights.items():
+            outputs["n" + kind + n] = a
+    scratch = {"b" + k: V(inputs[k].shape, F32) for k in held + ["s_counts"]}
+    for kind in ("ow_", "om_", "ov_"):
+        scratch.update({kind + n: V(a.shape, F32) for n, a in weights.items()})
+    whole = V(tokens.shape, BF16)
+    scratch.update(hold_x=whole, hold_g=whole)
+    scratch["hold_act"] = V(res["act_out"].shape, BF16)
+    scratch["hold_w"] = V(res["w_saved"].shape, BF16)
+    scratch.update(in_sem=dma((len(held) + 2 + 3 * FINISH_PARTS,)), out_sem=dma((12 + 2 * FINISH_PARTS,)))
     shapes = [jax.ShapeDtypeStruct(a.shape, a.dtype) for a in outputs.values()]
     names = list(inputs) + list(outputs) + ["type_counts"] + list(scratch)
     hbm = pl.BlockSpec(memory_space=pl.ANY)
-    out = pl.pallas_call(
-        lambda *refs: finish_kernel(BIG_COPIES, SimpleNamespace(**dict(zip(names, refs)))),
+    return pl.pallas_call(
+        lambda *refs: finish_kernel(SimpleNamespace(**dict(zip(names, refs)))),
         out_shape=tuple(shapes) + (jax.ShapeDtypeStruct((TYPES,), jnp.int32),),
         in_specs=[hbm] * len(inputs),
         out_specs=(hbm,) * len(outputs) + (pl.BlockSpec(memory_space=V),),
@@ -1202,7 +1242,6 @@
         compiler_params=pltpu.CompilerParams(vmem_limit_bytes=VMEM_BYTES),
         name="finish",
     )(*inputs.values())
-    return out
 
 
 def fused_body(
@@ -1224,11 +1263,13 @@
     square_norms,
 ):
     res = run_block(tokens, cotangent, lengths, labels, w_in.T, w_conv, w_out, norm_params)
+    names = ("in", "c0", "out", "norms")
     new = run_finish(
         res,
-        dict(zip(NAMES + ("norms",), (w_in.T, w_conv, w_out, norm_params))),
-        dict(zip(NAMES + ("norms",), (mean_w_in.T, mean_w_conv, mean_w_out, mean_norms))),
-        dict(zip(NAMES + ("norms",), (square_w_in.T, square_w_conv, square_w_out, square_norms))),
+        tokens,
+        dict(zip(names, (w_in.T, w_conv, w_out, norm_params))),
+        dict(zip(names, (mean_w_in.T, mean_w_conv, mean_w_out, mean_norms))),
+        dict(zip(names, (square_w_in.T, square_w_conv, square_w_out, square_norms))),
     )
     mixed, grad_tokens, *steps, counts = new
     for i in (0, 4, 8):

time: 176 us -> 151 us (0.86)
  Pallas kernels: 175 us -> 151 us
    pallas_call x1, Pallas kernels: 166 us -> 138 us  [run_block(): pl.pallas_call(lambda *refs: block_kernel(SimpleNamespace(**dict(zip(name...]
    pallas_call x1, Pallas kernels: 9.71 us -> 12.5 us  [run_finish(): pl.pallas_call(lambda *refs: finish_kernel(SimpleNamespace(**dict(zip(nam...]
where the time goes in v2:
time: 151 us
  Pallas kernels  151 us (100%)
    pallas_call x1, Pallas kernels, run_block(): pl.pallas_call(lambda *refs: block_kernel(SimpleNamespace(**dict(zip(name...  138 us
    pallas_call x1, Pallas kernels, run_finish(): pl.pallas_call(lambda *refs: finish_kernel(SimpleNamespace(**dict(zip(nam...  12.5 us

profile of v2, /device:TPU:0, one launch (start us, length us, event | category | flops | bytes accessed | tf_op | source)
XLA Modules:
  0.0 151.3 jit_solution(4710035217826870844)
XLA Ops:
  0.6 138.0 %residual_block.1 = (bf16[2048,640]{1,0:T(8,128)(2,1)}, bf16[2,2,2,160,640]{4,3,2,1,0:T(8,128)(2,1)}, bf16[2048,1280]{1,0:T(8,128)(2,1)}, f32[8,128]{1,0:T(8,128...) custom-call(s32[2]{0:T(128)} %refs_0_.1, ...), custom_call_target="tpu_custom_call" | custom-call | flops 45298483200 | bytes 20971520 | tf_op jit(solution)/shard_map/residual_block/pallas_call | solution.py:1100
  138.7 12.5 %finish.1 = (bf16[2048,1280]{1,0:T(8,128)(2,1)}, bf16[2048,1280]{1,0:T(8,128)(2,1)}, f32[80,320]{1,0:T(8,128)}, f32[5,160,80]{2,1,0:T(8,128)}, f32[160,160]{1,0:...) custom-call(bf16[2048,640]{1,0:T(8,128)(2,1)} %get-tuple-element.39., ...), custom_call_target="tpu_custom_call" | custom-call | tf_op jit(solution)/shard_map/finish/pallas_call | solution.py:1236

commit v3 on v2

--- a/solution.py
+++ b/solution.py
@@ -241,6 +241,8 @@
 HALO = (KERNEL_TAPS // 2) * DILATION_STRIDE
 GELU_SCALE, GELU_CUBE = 0.7978845608, 0.044715
 BLOCK = 256
+STRIP = 128
+FINE = 64
 UNROLL = 2
 
 
@@ -314,11 +316,16 @@
         self.xn = {"fsdp": f + 2 - 4 * self.x}
         self.yn = {"fsdp": f + 4 - 8 * self.y}
         self.zn = [{"dp": p} for p in self.ranks[1:]]
+        bits = [(m // 4, m // 2 % 2, m % 2) for m in range(1, PLANE)]
+        self.plane = [
+            4 * (self.oy if y else self.y) + 2 * (self.ox if x else self.x) + (self.oc if c else self.c)
+            for y, x, c in bits
+        ]
 
 
 def barrier(pc):
     sem = pltpu.get_barrier_semaphore()
-    peers = [pc.sib, pc.xn, pc.yn] + pc.zn
+    peers = [{"fsdp": p} for p in pc.plane] + pc.zn
     for p in peers:
         pl.semaphore_signal(sem, inc=1, device_id=p, device_id_type=MESH)
     pl.semaphore_wait(sem, len(peers))
@@ -497,7 +504,7 @@
     def add(self, at, ref, ref_at):
         for k in self.unit.taps:
             idx = self.unit.tap(k) + at
-            self.g[idx] = (self.g[idx].astype(F32) + ref[k + ref_at].astype(F32)).astype(BF16)
+            self.g[idx] = self.g[idx] + ref[k + ref_at]
 
     def step1(self):
         pc = self.pc
@@ -607,49 +614,74 @@
 
 
 class SmallSum:
-    SEMS = 7
-
-    def __init__(self, pc, acc, got, zgot, send, recv):
-        self.pc, self.acc, self.got, self.zgot, self.send, self.recv = pc, acc, got, zgot, send, recv
-
-    def stage(self, k):
-        pc = self.pc
-        return remote(
-            self.acc.at[k], self.got.at[k], self.send.at[k], self.recv.at[4 + k], (pc.sib, pc.xn, pc.yn)[k]
-        )
+    SEMS = 10
+
+    def __init__(self, pc, out, got, plane, zgot, send, recv):
+        self.pc, self.out, self.got, self.plane, self.zgot = pc, out, got, plane, zgot
+        self.send, self.recv = send, recv
+
+    def near(self, m):
+        pc = self.pc
+        p = pc.plane[m]
+        return remote(self.out.at[p], self.got.at[pc.f], self.send.at[m], self.recv.at[pc.f], {"fsdp": p})
+
+    def near_in(self, m):
+        p = self.pc.plane[m]
+        return remote(self.out.at[p], self.got.at[p], self.send.at[m], self.recv.at[p], {"fsdp": p})
 
     def z(self, j):
         pc = self.pc
-        return remote(self.acc.at[3], self.zgot.at[pc.d], self.send.at[2 + j], self.recv.at[pc.d], pc.zn[j - 1])
+        return remote(self.plane, self.zgot.at[pc.d], self.send.at[6 + j], self.recv.at[PLANE + pc.d], pc.zn[j - 1])
 
     def z_in(self, j):
         pc = self.pc
         p = pc.ranks[j]
-        return remote(self.acc.at[3], self.zgot.at[p], self.send.at[2 + j], self.recv.at[p], pc.zn[j - 1])
+        return remote(self.plane, self.zgot.at[p], self.send.at[6 + j], self.recv.at[PLANE + p], pc.zn[j - 1])
 
     def start(self):
-        self.stage(0).start()
-
-    def next(self, k):
-        self.stage(k).wait_recv()
-        self.acc[k + 1] = self.acc[k] + self.got[k]
-        if k < 2:
-            self.stage(k + 1).start()
-        else:
-            for j in range(1, DP_RANKS):
-                self.z(j).start()
+        for m in range(PLANE - 1):
+            self.near(m).start()
+
+    def along_z(self):
+        pc = self.pc
+        total = self.out[pc.f]
+        for m in range(PLANE - 1):
+            self.near_in(m).wait_recv()
+        for m in range(PLANE - 1):
+            total = total + self.got[pc.plane[m]]
+        self.plane[...] = total
+        for j in range(1, DP_RANKS):
+            self.z(j).start()
 
     def total(self):
+        total = self.plane[...]
         for j in range(1, DP_RANKS):
             self.z_in(j).wait_recv()
-        self.zgot[self.pc.d] = self.acc[3]
-        return (self.zgot[0] + self.zgot[1]) + (self.zgot[2] + self.zgot[3])
+            total = total + self.zgot[self.pc.ranks[j]]
+        return total
 
     def finish(self):
-        for k in range(3):
-            self.stage(k).wait_send()
+        for m in range(PLANE - 1):
+            self.near(m).wait_send()
         for j in range(1, DP_RANKS):
             self.z(j).wait_send()
+
+
+def lane_sum(v):
+    parts = [v[:, i : i + 128] for i in range(0, v.shape[1], 128)]
+    while len(parts) > 2:
+        pairs = [a + b for a, b in zip(parts[::2], parts[1::2])]
+        parts = pairs + parts[2 * len(pairs) :]
+    return jnp.sum(sum(p.astype(F32) for p in parts), axis=1, keepdims=True)
+
+
+def row_sum(v):
+    parts = [v[i : i + 16] for i in range(0, v.shape[0], 16)]
+    while len(parts) > 1:
+        pairs = [a + b for a, b in zip(parts[::2], parts[1::2])]
+        parts = pairs + parts[2 * len(pairs) :]
+    f = parts[0].astype(F32)
+    return f[0:8] + f[8:16]
 
 
 def norm_back(n, r, gain, bias, e, sums, row):
@@ -685,7 +717,8 @@
         return Scatter(pc, u, g, m.rcv_, m.r1a_, m.r1b_, m.r2a_, m.r2b_, m.zg_, m.zr_, m.ss_, m.sr_)
 
     norm_gather = NormGather(pc, r.nz, r.nw, r.ns, r.nr)
-    small = SmallSum(pc, r.sm_acc, r.sm_got, r.sm_z, r.sm_s, r.sm_r)
+    small = SmallSum(pc, r.sm_out, r.sm_got, r.sm_plane, r.sm_z, r.sm_s, r.sm_r)
+    count_sum = SmallSum(pc, r.ct_out, r.ct_got, r.ct_plane, r.ct_z, r.ct_s, r.ct_r)
 
     load_x = pltpu.make_async_copy(r.tokens, x, r.io.at[0])
     load_cot = pltpu.make_async_copy(r.cot_in, cot, r.io.at[1])
@@ -724,16 +757,18 @@
     valid = place < 0
     for s in range(slots):
         valid = valid | ((place >= s * seq) & (place < s * seq + r.lens[s]))
-    lane = lax.broadcasted_iota(jnp.int32, (1, inner), 1)
-    counts = jnp.zeros((1, inner), F32)
+    lane = lax.broadcasted_iota(jnp.int32, (8, 128), 1)
+    counts = jnp.zeros((8, 128), F32)
     for c in range(TYPES):
         hits = jnp.sum(jnp.where(valid & (lab == c), 1.0, 0.0), keepdims=True)
         counts = counts + jnp.where(lane == c, hits, 0.0)
-    small.acc[0, 8:9, :] = counts
+    for f in range(PLANE):
+        r.ct_out[f] = counts
+    count_sum.start()
 
     load_x.wait()
     load_cot.start()
-    strip = BLOCK // 2
+    strip = STRIP
     strips = rows // strip
 
     def first_stats(i):
@@ -751,8 +786,8 @@
             strips * 3 // 4: [get_c0.start, lambda: norm_gather.next(1)],
         },
     )
+    get_in.own()
     norm_gather.next(2)
-    get_in.own()
     r.norms[...] = norm_gather.whole(cols)
     norms = r.norms
     gain_a = jnp.concatenate([norms[0:1, :], norms[1:2, :]], axis=1)
@@ -838,14 +873,15 @@
         total_blocks,
         second,
         second_rest,
-        {0: [get_c0.from_x, get_c0.from_y], 1: [get_c1.own, get_out.start], loop_end: [get_c0.from_diagonal]},
-    )
+        {loop_end // 2: [get_c1.own, get_out.start], loop_end: [get_c0.from_x, get_c0.from_y]},
+    )
+    get_c0.from_diagonal()
     get_c1.from_x()
     get_c1.from_y()
+    get_c0.from_sibling()
+    get_c1.from_diagonal()
+    get_c1.from_sibling()
     get_out.own()
-    get_c1.from_diagonal()
-    get_c0.from_sibling()
-    get_c1.from_sibling()
 
     def conv_rows():
         v = [w_conv[k].reshape(inner, inner) for k in range(KERNEL_TAPS)]
@@ -866,7 +902,12 @@
             total_blocks,
             third,
             third_rest,
-            {0: [get_out.from_x, get_out.from_y], 1: [get_out.from_diagonal], loop_end: [get_out.from_sibling]},
+            {
+                0: [count_sum.along_z],
+                loop_end // 2: [get_out.from_x, get_out.from_y],
+                loop_end - 1: [get_out.from_diagonal],
+                loop_end: [get_out.from_sibling],
+            },
         )
         save_act.start()
         save_w.start()
@@ -960,25 +1001,44 @@
         def out_copy(at):
             return pltpu.make_async_copy(cot.at[at, :], r.grad_tokens.at[at, :], r.io.at[4])
 
-        def eighth(i):
-            at = block(i, BLOCK)
-            e = dot_nn(grad_a[at, :], flat(w_in))
-            back = norm_back(x[at, :].astype(F32), scale[at, 0:1], gain_a, bias_a, e, sums, 0)
-            cot[at, :] = (cot[at, :].astype(F32) + back).astype(BF16)
-            out_copy(at).start()
-
-        loop(
+        low_gain, low_bias = gain_a.astype(BF16), bias_a.astype(BF16)
+
+        def eighth(j):
+            return dot_nn(grad_a[block(j, BLOCK), :], flat(w_in))
+
+        def eighth_rest(j, h):
+            d_gain = d_bias = None
+            for at in range(0, BLOCK, FINE):
+                here = pl.ds(pl.multiple_of(j * BLOCK + at, FINE), FINE)
+                n = x[here, :]
+                z = n * low_gain + low_bias
+                zz = z * z
+                t = jnp.tanh(z * (BF16(GELU_SCALE) + BF16(GELU_SCALE * GELU_CUBE) * zz))
+                slope = z * (BF16(0.5 * GELU_SCALE) + BF16(1.5 * GELU_SCALE * GELU_CUBE) * zz)
+                dz = h[at : at + FINE].astype(BF16) * ((BF16(0.5) + BF16(0.5) * t) + (slope - (t * t) * slope))
+                a, b = row_sum(dz * n), row_sum(dz)
+                d_gain, d_bias = (a, b) if d_gain is None else (d_gain + a, d_bias + b)
+                dn = dz * low_gain
+                m1 = lane_sum(dn) * (1.0 / width)
+                m2 = lane_sum(dn * n) * (1.0 / width)
+                m1, m2, rs = (jnp.broadcast_to(v, n.shape).astype(BF16) for v in (m1, m2, scale[here, 0:1]))
+                cot[here, :] = cot[here, :] + rs * (dn - m1 - n * m2)
+            sums[0:1, :] += jnp.sum(d_gain, axis=0, keepdims=True)
+            sums[1:2, :] += jnp.sum(d_bias, axis=0, keepdims=True)
+            out_copy(block(j, BLOCK)).start()
+
+        skewed(
             total_blocks,
             eighth,
+            eighth_rest,
             {
                 0: [put_in.step1, put_c1.step3],
-                2: [lambda: put_c0.step4(r.s_c0)],
-                3: [put_in.step2],
-                4: [lambda: put_c1.step4(r.s_c1)],
-                6: [put_in.step3],
+                1: [lambda: put_c0.step4(r.s_c0)],
+                2: [put_in.step2],
+                loop_end: [lambda: put_c1.step4(r.s_c1), put_in.step3],
             },
         )
-        small.acc[0, 0:8] = jnp.concatenate(
+        mine = jnp.concatenate(
             [
                 sums[0:1, 0:inner],
                 sums[0:1, inner : 2 * inner],
@@ -988,20 +1048,18 @@
             ],
             axis=0,
         )
+        for f in range(PLANE):
+            r.sm_out[f, :, 0:cols] = mine[:, f * cols : (f + 1) * cols]
         small.start()
-        for k in range(3):
-            small.next(k)
+        r.s_counts[...] = count_sum.total()
+        small.along_z()
         total = small.total()
-        r.s_counts[...] = total[8:16, 0:128]
-        mine = jnp.zeros((8, cols), F32)
-        for f in range(PLANE):
-            mine = mine + jnp.where(pc.f == f, total[0:8, f * cols : (f + 1) * cols], 0.0)
         pair = jnp.zeros((2, cols), F32)
         for i in range(DP_RANKS):
-            pair = pair + jnp.where(pc.d == i, mine[2 * i : 2 * i + 2], 0.0)
+            pair = pair + jnp.where(pc.d == i, total[2 * i : 2 * i + 2, 0:cols], 0.0)
         r.s_norms[...] = pair
         put_in.step4(r.s_in)
-        for c in (put_in, put_c0, put_c1, put_out, small):
+        for c in (put_in, put_c0, put_c1, put_out, small, count_sum):
             c.finish()
 
         def eighth_end(_):
@@ -1068,12 +1126,18 @@
         nw=V((2, 2, 2, 8, 128), F32),
         ns=dma((NormGather.SEMS,)),
         nr=dma((NormGather.SEMS,)),
-        sm_acc=V((4, 16, inner), F32),
-        sm_got=V((3, 16, inner), F32),
-        sm_z=V((DP_RANKS, 16, inner), F32),
-        sm_s=dma((SmallSum.SEMS,)),
-        sm_r=dma((SmallSum.SEMS,)),
-    )
+    )
+    tile = (8, 128)
+    for k in ("sm_", "ct_"):
+        shapes = (
+            V((PLANE,) + tile, F32),
+            V((PLANE,) + tile, F32),
+            V(tile, F32),
+            V((DP_RANKS,) + tile, F32),
+            dma((SmallSum.SEMS,)),
+            dma((PLANE + DP_RANKS,)),
+        )
+        scratch.update(zip([k + n for n in ("out", "got", "plane", "z", "s", "r")], shapes))
     for u in UNITS:
         lead = (u.count,) if u.count else ()
         h, lanes = (cols, width) if u.name == "in" else (h_out, inner) if u.name == "out" else (cols, inner)
@@ -1123,13 +1187,14 @@
         loads[k] = pltpu.make_async_copy(src, dst, r.in_sem.at[len(loads)])
         loads[k].start()
 
-    load("w", r.w_saved, r.hold_w)
     parts = [pl.ds(i * rows, rows) for i in range(FINISH_PARTS)]
     for i, at in enumerate(parts):
         load(("a", i), r.act_out.at[at, :], r.hold_act.at[at, :])
         load(("t", i), r.tokens.at[at, :], r.hold_x.at[at, :])
+        if i == 0:
+            load("w", r.w_saved, r.hold_w)
         load(("g", i), r.grad_tokens.at[at, :], r.hold_g.at[at, :])
-        if i == 0:
+        if i == 1:
             for n in STEP_ORDER:
                 load("s_" + n, getattr(r, "s_" + n), getattr(r, "bs_" + n))
                 for kind in ("w_", "m_", "v_"):
@@ -1196,14 +1261,14 @@
         store(r.hold_x.at[at, :], r.new_mixed.at[at, :])
         loads[("g", i)].wait()
         store(r.hold_g.at[at, :], r.new_grad_tokens.at[at, :])
-        if i < len(others):
-            others[i]()
+        if 0 <= i - 2 < len(others):
+            others[i - 2]()
     for c in stores:
         c.wait()
 
 
 STEP_ORDER = ("c0", "c1", "in", "out", "norms")
-FINISH_PARTS = 4
+FINISH_PARTS = 8
 
 
 def run_finish(res, tokens, weights, means, squares):

time: 151 us -> 144 us (0.954)
  Pallas kernels: 151 us -> 143 us
    pallas_call x1, Pallas kernels: 138 us -> 131 us  [run_block(): pl.pallas_call(lambda *refs: block_kernel(SimpleNamespace(**dict(zip(name...]
where the time goes in v3:
time: 144 us
  Pallas kernels  143 us (99%)
    pallas_call x1, Pallas kernels, run_block(): pl.pallas_call(lambda *refs: block_kernel(SimpleNamespace(**dict(zip(name...  131 us
    pallas_call x1, Pallas kernels, run_finish(): pl.pallas_call(lambda *refs: finish_kernel(SimpleNamespace(**dict(zip(nam...  12.2 us

profile of v3, /device:TPU:0, one launch (start us, length us, event | category | flops | bytes accessed | tf_op | source)
XLA Modules:
  0.0 144.3 jit_solution(17145875948482156334)
XLA Ops:
  0.6 131.3 %residual_block.1 = (bf16[2048,640]{1,0:T(8,128)(2,1)}, bf16[2,2,2,160,640]{4,3,2,1,0:T(8,128)(2,1)}, bf16[2048,1280]{1,0:T(8,128)(2,1)}, f32[8,128]{1,0:T(8,128...) custom-call(s32[2]{0:T(128)} %refs_0_.1, ...), custom_call_target="tpu_custom_call" | custom-call | flops 45298483200 | bytes 20971520 | tf_op jit(solution)/shard_map/residual_block/pallas_call | solution.py:1164
  131.9 12.2 %finish.1 = (bf16[2048,1280]{1,0:T(8,128)(2,1)}, bf16[2048,1280]{1,0:T(8,128)(2,1)}, f32[80,320]{1,0:T(8,128)}, f32[5,160,80]{2,1,0:T(8,128)}, f32[160,160]{1,0:...) custom-call(bf16[2048,640]{1,0:T(8,128)(2,1)} %get-tuple-element.39., ...), custom_call_target="tpu_custom_call" | custom-call | tf_op jit(solution)/shard_map/finish/pallas_call | solution.py:1301

commit v4 on v3

--- a/solution.py
+++ b/solution.py
@@ -905,15 +905,11 @@
             {
                 0: [count_sum.along_z],
                 loop_end // 2: [get_out.from_x, get_out.from_y],
-                loop_end - 1: [get_out.from_diagonal],
-                loop_end: [get_out.from_sibling],
+                loop_end: [get_out.from_diagonal],
             },
         )
         save_act.start()
-        save_w.start()
         load_cot.wait()
-        for c in [norm_gather] + pull:
-            c.finish()
 
         tall = r.g_out.shape[3]
 
@@ -925,6 +921,10 @@
 
         for lo in range(0, width, chunk):
             once(out_grad, lo)
+        get_out.from_sibling()
+        save_w.start()
+        for c in [norm_gather] + pull:
+            c.finish()
         put_out = scatter(UNITS[3], r.g_out)
         put_out.start()
 
@@ -938,7 +938,7 @@
             shifted_store(g_even, g_odd, j, back)
             back_t[:, at] = back.astype(BF16).T
 
-        skewed(total_blocks, fourth, fourth_rest, {0: [put_out.step1], 2: [put_out.step2]})
+        skewed(total_blocks, fourth, fourth_rest, {0: [put_out.step1], loop_end: [put_out.step2]})
 
     pl.run_scoped(middle, pltpu.VMEM((rows, inner), BF16))
     put_out = scatter(UNITS[3], r.g_out)
@@ -958,7 +958,7 @@
 
         for k in range(KERNEL_TAPS):
             once(conv_grad, k)
-            if k == 0:
+            if k == 1:
                 put_out.step3()
             if k == 2:
                 put_c0.start()
@@ -1033,9 +1033,8 @@
             eighth_rest,
             {
                 0: [put_in.step1, put_c1.step3],
-                1: [lambda: put_c0.step4(r.s_c0)],
                 2: [put_in.step2],
-                loop_end: [lambda: put_c1.step4(r.s_c1), put_in.step3],
+                loop_end: [put_in.step3],
             },
         )
         mine = jnp.concatenate(
@@ -1052,7 +1051,9 @@
             r.sm_out[f, :, 0:cols] = mine[:, f * cols : (f + 1) * cols]
         small.start()
         r.s_counts[...] = count_sum.total()
+        put_c0.step4(r.s_c0)
         small.along_z()
+        put_c1.step4(r.s_c1)
         total = small.total()
         pair = jnp.zeros((2, cols), F32)
         for i in range(DP_RANKS):
@@ -1193,14 +1194,16 @@
         load(("t", i), r.tokens.at[at, :], r.hold_x.at[at, :])
         if i == 0:
             load("w", r.w_saved, r.hold_w)
-        load(("g", i), r.grad_tokens.at[at, :], r.hold_g.at[at, :])
-        if i == 1:
+        if i > 0:
+            load(("g", i - 1), r.grad_tokens.at[parts[i - 1], :], r.hold_g.at[parts[i - 1], :])
+        if i == 3:
             for n in STEP_ORDER:
                 load("s_" + n, getattr(r, "s_" + n), getattr(r, "bs_" + n))
                 for kind in ("w_", "m_", "v_"):
                     if n != "c1":
                         load(kind + n, getattr(r, kind + n), getattr(r, "b" + kind + n))
             load("n", r.s_counts, r.bs_counts)
+    load(("g", len(parts) - 1), r.grad_tokens.at[parts[-1], :], r.hold_g.at[parts[-1], :])
     stores = []
 
     def store(src, dst):
@@ -1259,10 +1262,13 @@
         hid = dot_nt(r.hold_act[at, :], w.reshape(PLANE * w.shape[3], w.shape[4]))
         r.hold_x[at, :] = (r.hold_x[at, :].astype(F32) + hid).astype(BF16)
         store(r.hold_x.at[at, :], r.new_mixed.at[at, :])
-        loads[("g", i)].wait()
-        store(r.hold_g.at[at, :], r.new_grad_tokens.at[at, :])
-        if 0 <= i - 2 < len(others):
-            others[i - 2]()
+        if i > 0:
+            loads[("g", i - 1)].wait()
+            store(r.hold_g.at[parts[i - 1], :], r.new_grad_tokens.at[parts[i - 1], :])
+        if 0 <= i - 4 < len(others):
+            others[i - 4]()
+    loads[("g", len(parts) - 1)].wait()
+    store(r.hold_g.at[parts[-1], :], r.new_grad_tokens.at[parts[-1], :])
     for c in stores:
         c.wait()
 

time: 144 us -> 142 us (0.986)
  Pallas kernels: 143 us -> 141 us
    pallas_call x1, Pallas kernels: 131 us -> 130 us  [run_block(): pl.pallas_call(lambda *refs: block_kernel(SimpleNamespace(**dict(zip(name...]
where the time goes in v4:
time: 142 us
  Pallas kernels  141 us (99%)
    pallas_call x1, Pallas kernels, run_block(): pl.pallas_call(lambda *refs: block_kernel(SimpleNamespace(**dict(zip(name...  130 us
    pallas_call x1, Pallas kernels, run_finish(): pl.pallas_call(lambda *refs: finish_kernel(SimpleNamespace(**dict(zip(nam...  11.7 us

profile of v4, /device:TPU:0, one launch (start us, length us, event | category | flops | bytes accessed | tf_op | source)
XLA Modules:
  0.0 142.3 jit_solution(5470267425207582542)
XLA Ops:
  0.6 129.7 %residual_block.1 = (bf16[2048,640]{1,0:T(8,128)(2,1)}, bf16[2,2,2,160,640]{4,3,2,1,0:T(8,128)(2,1)}, bf16[2048,1280]{1,0:T(8,128)(2,1)}, f32[8,128]{1,0:T(8,128...) custom-call(s32[2]{0:T(128)} %refs_0_.1, ...), custom_call_target="tpu_custom_call" | custom-call | flops 45298483200 | bytes 20971520 | tf_op jit(solution)/shard_map/residual_block/pallas_call | solution.py:1165
  130.4 11.7 %finish.1 = (bf16[2048,1280]{1,0:T(8,128)(2,1)}, bf16[2048,1280]{1,0:T(8,128)(2,1)}, f32[80,320]{1,0:T(8,128)}, f32[5,160,80]{2,1,0:T(8,128)}, f32[160,160]{1,0:...) custom-call(bf16[2048,640]{1,0:T(8,128)(2,1)} %get-tuple-element.39., ...), custom_call_target="tpu_custom_call" | custom-call | tf_op jit(solution)/shard_map/finish/pallas_call | solution.py:1307
